TPU v7x, 128 devices: a whole 4x4x4 slice. The times are simulated.
128 devices in a mesh: ctx: 32 (over z, y_hi, x), dp: 4 (over y_lo, core).
Axes of the slice: x: 4, y: 4 (y_hi: 2, y_lo: 2; y = y_hi * 2 + y_lo), z: 4, core: 2. Of those that a mesh axis runs over, the one named last changes fastest.
Arguments:
- queries: bfloat16 [32768, 1024], P(('dp', 'ctx')), parts along dimension 0, may hold values from -6 to 6
- keys: bfloat16 [32768, 128], P(('dp', 'ctx')), parts along dimension 0, may hold values from -6 to 6
- values: bfloat16 [32768, 128], P(('dp', 'ctx')), parts along dimension 0, may hold values from -6 to 6
- outputs: bfloat16 [32768, 1024], P(('dp', 'ctx')), parts along dimension 0, may hold values from -6 to 6
- out_grad: bfloat16 [32768, 1024], P(('dp', 'ctx')), parts along dimension 0, may hold values from -6 to 6
- lse: float32 [8, 32768], P(None, ('dp', 'ctx')), parts along dimension 1, as said below
- block_order: int32 [256], P('dp'), parts along dimension 0, may hold values from 0 to 63, as said below
- doc_lengths: int32 [64], P('dp'), parts along dimension 0, may hold values from 1 to 4096, as said below
Outputs:
- query_grad: bfloat16 [32768, 1024], P(('dp', 'ctx')), parts along dimension 0
- key_grad: bfloat16 [32768, 128], P(('dp', 'ctx')), parts along dimension 0
- value_grad: bfloat16 [32768, 128], P(('dp', 'ctx')), parts along dimension 0
There are 4 independent parts, one for each index of `dp`. A program takes and returns all parts, laid end to end along the dimension named above; each array names one. Nothing has to cross between parts.
Inputs may be any that keep to these rules, and one draw needn't show every extreme that they name: `block_order`: A permutation of the 64 sequence blocks. `doc_lengths`: positive lengths summing to 8192; the longest document has exactly 4096 tokens. `lse`: each entry exceeds the logarithm of the number of keys that its query may attend to.
All inputs are finite; a program needn't handle non-finite values.
Results may differ from a plain program's by a relative error of at most 0.0052.
Values may be sent and summed in bfloat16 or wider, within the bound.
A program may use at most 64 MiB of HBM per device.

v0:
```python
import math

import jax
import jax.numpy as jnp
from jax import lax
from jax.sharding import PartitionSpec as P


def local(queries, keys, values, outputs, out_grad, lse, block_order, doc_lengths):
    tokens = queries.shape[0]
    heads = lse.shape[0]
    width = keys.shape[1]
    block = tokens // 2
    scale = width ** (-0.5)
    device = lax.axis_index("ctx")
    ends = jnp.cumsum(doc_lengths)
    block_ids = jnp.arange(block_order.shape[0], dtype=jnp.int32)

    def locate(rows):
        which = rows // block
        base = jnp.sum(
            jnp.where(which[:, None] == block_ids[None, :], block_order[None, :], 0), axis=1
        )
        places = base * block + rows % block
        docs = jnp.sum((ends[None, :] <= places[:, None]).astype(jnp.int32), axis=1)
        return (places, docs)

    query_pos, query_doc = locate(device * tokens + jnp.arange(tokens, dtype=jnp.int32))
    query_rows = queries.reshape(tokens * heads, width)
    grad_rows = out_grad.reshape(tokens * heads, width)
    stats = lse.T.reshape(-1)
    delta = jnp.sum(
        (out_grad.astype(jnp.float32) * outputs.astype(jnp.float32)).reshape(tokens, heads, width),
        axis=2,
    ).reshape(-1)

    def tile(key_part, value_part, start):
        count = key_part.shape[0]
        key_pos, key_doc = locate(start + jnp.arange(count, dtype=jnp.int32))
        allowed_tok = (key_pos[None, :] <= query_pos[:, None]) & (
            key_doc[None, :] == query_doc[:, None]
        )
        allowed = jnp.repeat(allowed_tok, heads, axis=0)
        score = scale * jnp.dot(query_rows, key_part.T, preferred_element_type=jnp.float32)
        prob = jnp.where(allowed, jnp.exp(score - stats[:, None]), jnp.float32(0.0))
        prob_b = prob.astype(jnp.bfloat16)
        dprob = jnp.dot(grad_rows, value_part.T, preferred_element_type=jnp.float32)
        dscore = (prob * (dprob - delta[:, None])).astype(jnp.bfloat16)
        query_term = jnp.dot(dscore, key_part, preferred_element_type=jnp.float32)
        key_term = jnp.einsum("rk,rd->kd", dscore, query_rows, preferred_element_type=jnp.float32)
        value_term = jnp.einsum("rk,rd->kd", prob_b, grad_rows, preferred_element_type=jnp.float32)
        return (query_term, key_term, value_term)

    query_acc = jnp.zeros((tokens * heads, width), jnp.float32)
    key_part = lax.all_gather(keys, "ctx", axis=0, tiled=True)
    value_part = lax.all_gather(values, "ctx", axis=0, tiled=True)
    count = key_part.shape[0]
    step_rows = math.gcd(count, 512)

    def visit(index, carry):
        query_acc, key_acc, value_acc = carry
        offset = index * step_rows
        key_slab = lax.dynamic_slice_in_dim(key_part, offset, step_rows, 0)
        value_slab = lax.dynamic_slice_in_dim(value_part, offset, step_rows, 0)
        query_term, key_term, value_term = tile(key_slab, value_slab, offset)
        key_acc = lax.dynamic_update_slice_in_dim(key_acc, key_term, offset, 0)
        value_acc = lax.dynamic_update_slice_in_dim(value_acc, value_term, offset, 0)
        return (query_acc + query_term, key_acc, value_acc)

    empty_rows = jnp.zeros((count, width), jnp.float32)
    query_term, key_term, value_term = lax.fori_loop(
        0,
        count // step_rows,
        visit,
        (jnp.zeros((tokens * heads, width), jnp.float32), empty_rows, empty_rows),
    )
    key_all = key_term
    value_all = value_term
    query_acc, key_all, value_all = (query_term, key_all, value_all)
    key_mine, value_mine = (
        lax.psum_scatter(key_all, "ctx", scatter_dimension=0, tiled=True),
        lax.psum_scatter(value_all, "ctx", scatter_dimension=0, tiled=True),
    )
    query_grad = (scale * query_acc).astype(jnp.bfloat16).reshape(tokens, heads * width)
    key_grad = (scale * key_mine).astype(jnp.bfloat16)
    value_grad = value_mine.astype(jnp.bfloat16)
    return (query_grad, key_grad, value_grad)


def solution(mesh):
    return jax.shard_map(
        local,
        mesh=mesh,
        in_specs=(
            P(("dp", "ctx"), None),
            P(("dp", "ctx"), None),
            P(("dp", "ctx"), None),
            P(("dp", "ctx"), None),
            P(("dp", "ctx"), None),
            P(None, ("dp", "ctx")),
            P("dp"),
            P("dp"),
        ),
        out_specs=(P(("dp", "ctx"), None), P(("dp", "ctx"), None), P(("dp", "ctx"), None)),
        check_vma=False,
    )
```

profile of v0, /device:TPU:0, one launch (start us, length us, event | category | flops | bytes accessed | tf_op | source)
XLA Modules:
  0.0 734.2 jit_solution(7991751485762508101)
XLA Ops:
  13.7 70.8 %all-gather.3.cloned.1.call-done = bf16[8192,128]{1,0:T(8,128)(2,1)} async-done(((bf16[256,128]{1,0:T(8,128)(2,1)}), bf16[8192,128]{1,0:T(8,128)(2,1)}) %all-gather.3.cloned.1.call-update) | async-done | bytes 2097168 | tf_op jit(solution)/shard_map/all_gather | solution.py:55
  84.5 70.7 %all-gather.5.cloned.1.call-done = bf16[8192,128]{1,0:T(8,128)(2,1)} async-done(((bf16[256,128]{1,0:T(8,128)(2,1)}), bf16[8192,128]{1,0:T(8,128)(2,1)}) %all-gather.5.cloned.1.call-update) | async-done | bytes 2097168 | tf_op jit(solution)/shard_map/all_gather | solution.py:56
  155.2 2.2 broadcast_in_dim.102
  157.4 2.2 broadcast_in_dim.102.clone
  159.6 187.6 %while.21 = (s32[]{:T(128)}, f32[2048,128]{1,0:T(8,128)}, f32[8192,128]{1,0:T(8,128)}, f32[8192,128]{1,0:T(8,128)}, s32[64]{0:T(128)S(1)}, /*index=5*/s32[256]{0...) while((s32[]{:T(128)}, f32[2048,128]{1,0:T(8,128)}, ...), condition=%wide.wide.region_7.8_spmd.clone, body=%wide.wide.region_4.7_spmd.clone.sunk | while | flops 1350572032 | bytes 28480072 | solution.py:71
  161.7 2.1 bitcast_select_fusion.3
  163.8 1.6 fusion.63
  168.2 2.7 convolution_add_fusion.3
  173.0 2.1 bitcast_select_fusion.3
  175.1 1.6 fusion.63
  179.6 3.1 convolution_add_fusion.3
  184.7 2.1 bitcast_select_fusion.3
  186.8 1.6 fusion.63
  191.3 3.1 convolution_add_fusion.3
  196.5 2.1 bitcast_select_fusion.3
  198.6 1.6 fusion.63
  201.7 1.4 fusion.64
  203.1 3.1 convolution_add_fusion.3
  208.3 2.1 bitcast_select_fusion.3
  210.4 1.6 fusion.63
  212.0 1.4 convolution_dynamic-update-slice_fusion.3
  214.9 3.1 convolution_add_fusion.3
  220.0 2.1 bitcast_select_fusion.3
  222.1 1.6 fusion.63
  225.2 1.4 fusion.64
  226.6 3.1 convolution_add_fusion.3
  231.8 2.1 bitcast_select_fusion.3
  233.9 1.6 fusion.63
  238.4 3.1 convolution_add_fusion.3
  243.5 2.1 bitcast_select_fusion.3
  245.6 1.6 fusion.63
  250.1 3.1 convolution_add_fusion.3
  255.3 2.1 bitcast_select_fusion.3
  257.4 1.6 fusion.63
  259.0 1.4 convolution_dynamic-update-slice_fusion.3
  261.9 3.1 convolution_add_fusion.3
  267.1 2.1 bitcast_select_fusion.3
  269.2 1.6 fusion.63
  273.6 3.1 convolution_add_fusion.3
  278.8 2.1 bitcast_select_fusion.3
  280.9 1.6 fusion.63
  284.0 1.4 fusion.64
  285.4 3.1 convolution_add_fusion.3
  290.6 2.1 bitcast_select_fusion.3
  292.7 1.6 fusion.63
  294.3 1.4 convolution_dynamic-update-slice_fusion.3
  297.2 3.1 convolution_add_fusion.3
  302.3 2.1 bitcast_select_fusion.3
  304.4 1.6 fusion.63
  306.1 1.4 convolution_dynamic-update-slice_fusion.3
  308.9 3.1 convolution_add_fusion.3
  314.1 2.1 bitcast_select_fusion.3
  316.2 1.6 fusion.63
  320.7 3.1 convolution_add_fusion.3
  325.8 2.1 bitcast_select_fusion.3
  327.9 1.6 fusion.63
  332.4 3.1 convolution_add_fusion.3
  337.5 2.1 bitcast_select_fusion.3
  339.6 1.6 fusion.63
  344.1 3.1 convolution_add_fusion.3
  349.6 187.3 %reduce-scatter.5.cloned.1.call-done = f32[256,128]{1,0:T(8,128)} async-done(((f32[8192,128]{1,0:T(8,128)}), f32[256,128]{1,0:T(8,128)}) %reduce-scatter.5.cloned.1.call-update) | async-done | bytes 131088 | tf_op jit(solution)/shard_map/reduce_scatter | solution.py:82
  536.8 1.5 convert_element_type.53
  538.4 187.7 %reduce-scatter.3.cloned.1.call-done = f32[256,128]{1,0:T(8,128)} async-done(((f32[8192,128]{1,0:T(8,128)}), f32[256,128]{1,0:T(8,128)}) %reduce-scatter.3.cloned.1.call-update) | async-done | bytes 131088 | tf_op jit(solution)/shard_map/reduce_scatter | solution.py:81
  726.1 1.5 multiply_convert_fusion.1
  (175 shorter events, 76.6 us)
Async XLA Ops:
  7.2 5.8 copy-start.5
  7.2 6.0 copy-start.2
  7.2 6.3 copy-start.4
  7.2 77.3 %all-gather.3.cloned.1.call-start = ((), (), s32[]{:S(2)}) async-start(), calls=%async_computation.2 | async-start | bytes 2162688 | tf_op jit(solution)/shard_map/all_gather | solution.py:55
  7.9 147.3 %all-gather.5.cloned.1.call-start = ((), (), s32[]{:S(2)}) async-start(), calls=%async_computation.3 | async-start | bytes 2162688 | tf_op jit(solution)/shard_map/all_gather | solution.py:56
  8.7 528.1 %reduce-scatter.5.cloned.1.call-start = ((), (), s32[]{:S(2)}) async-start(), calls=%async_computation.5 | async-start | bytes 4325376 | tf_op jit(solution)/shard_map/reduce_scatter | solution.py:82
  12.8 146.8 %copy-start.1 = (f32[256,8]{1,0:T(8,128)}, f32[256,8]{1,0:T(8,128)S(1)}, u32[]{:S(2)}) copy-start(f32[256,8]{1,0:T(8,128)S(1)} %reduce_sum.61) | copy-start | bytes 24580
  13.1 146.5 %copy-start.3 = (f32[8,256]{0,1:T(8,128)}, f32[8,256]{0,1:T(8,128)S(1)}, u32[]{:S(2)}) copy-start(f32[8,256]{0,1:T(8,128)S(1)} %copy.17) | copy-start | bytes 24580
  347.2 1.2 copy-start
  347.3 378.8 %reduce-scatter.3.cloned.1.call-start = ((), (), s32[]{:S(2)}) async-start(), calls=%async_computation.4 | async-start | bytes 4325376 | tf_op jit(solution)/shard_map/reduce_scatter | solution.py:81
Sparse Core Ops, SparseCore 0:
  11.0 73.3 all-gather.2
  87.4 67.6 all-gather.4
  347.4 189.4 reduce-scatter.4
  539.1 186.9 reduce-scatter.2
where the time goes:
time: 735 us; the launch traced here: 734 us
  waiting for transfers between devices  518 us (70%)
  matrix products  154 us (21%)
  local copies, waits for them, and re-layouts  35.1 us (5%)
  between operations  13.9 us (2%)
  other arithmetic  11.4 us (2%)
    reduce_scatter x1, waiting for transfers between devices, local(): lax.psum_scatter(key_all, 'ctx', scatter_dimension=0, tiled=True)  188 us
    reduce_scatter x1, waiting for transfers between devices, local(): lax.psum_scatter(value_all, 'ctx', scatter_dimension=0, tiled=True)  187 us
    all_gather x1, waiting for transfers between devices, local(): key_part = lax.all_gather(keys, 'ctx', axis=0, tiled=True)  70.8 us
    all_gather x1, waiting for transfers between devices, local(): value_part = lax.all_gather(values, 'ctx', axis=0, tiled=True)  70.7 us
    dot_general x16, matrix products, tile(): query_term = jnp.dot(dscore, key_part, preferred_element_type=jnp.float32)  49.2 us
    dot_general x16, matrix products, tile(): jnp.dot(query_rows, key_part.T, preferred_element_type=jnp.float32)  33.4 us
    reshape x32, local copies, waits for them, and re-layouts, tile(): allowed = jnp.repeat(allowed_tok, heads, axis=0)  26.3 us
    dot_general x16, matrix products, tile(): dprob = jnp.dot(grad_rows, value_part.T, preferred_element_type=jnp.float32)  26.2 us
  transfers between devices with their start and end apart: 4, of which 4 were waited for; matrix products, arithmetic and copies ran while one was open for 1% of the time, Pallas kernels for 0%

commit v1 on v0

v1 whole, which is shorter than its diff:
```python
import functools

import jax
import jax.numpy as jnp
from jax import lax
from jax.experimental import pallas as pl
from jax.experimental.pallas import tpu as pltpu
from jax.sharding import PartitionSpec as P

BF = jnp.bfloat16
F32 = jnp.float32
I32 = jnp.int32
MESH = pl.DeviceIdType.MESH
VM = pl.BlockSpec(memory_space=pltpu.VMEM)
SM = pl.BlockSpec(memory_space=pltpu.SMEM)

RING = 4
PLANE = RING * RING
T = 256
B = 128
H = 8
D = 128
VMEM_LIMIT = 56 * 2**20


def dot(a, b, ca, cb):
    return lax.dot_general(a, b, (((ca,), (cb,)), ((), ())), preferred_element_type=F32)


def coords():
    me = lax.axis_index("ctx")
    return me // 8, (me // 4) % 2, me % 4


def ident(z, y, x):
    return {"ctx": z * 8 + y * 4 + x}


def step_of(v, d):
    return lax.rem(v + d, RING)


def greet(z, y, x, pair):
    barrier = pltpu.get_barrier_semaphore()
    others = [ident(z, y, step_of(x, d)) for d in (1, 2, 3)]
    others += [ident(step_of(z, d), y, x) for d in (1, 2, 3)]
    if pair:
        others.append(ident(z, 1 - y, x))
    for other in others:
        pl.semaphore_signal(barrier, inc=1, device_id=other, device_id_type=MESH)
    pl.semaphore_wait(barrier, len(others))


def gather_kernel(
    k_ref, v_ref, g_ref, o_ref, lse_ref, ka, va, delta, pair_delta, pair_lse,
    own_sem, s1, r1, s2, r2, ps, pr,
):
    z, y, x = coords()
    greet(z, y, x, True)
    here = z * RING + x
    pair = ident(z, 1 - y, x)

    def send(src, dst, ssem, rsem, to):
        copy = pltpu.make_async_remote_copy(
            src_ref=src, dst_ref=dst, send_sem=ssem, recv_sem=rsem, device_id=to, device_id_type=MESH
        )
        copy.start()
        return copy

    srcs, alls = (k_ref, v_ref), (ka, va)

    def first_peer(a, d):
        return ident(z, y, step_of(x, d)) if a == 0 else ident(step_of(z, d), y, x)

    def second_peer(a, d):
        return first_peer(1 - a, d)

    def slot_from(a, s):
        return z * RING + step_of(x, RING - s) if a == 0 else step_of(z, RING - s) * RING + x

    first, second = {}, {}
    for a in (0, 1):
        for d in (1, 3, 2):
            first[a, d] = send(srcs[a], alls[a].at[here], s1.at[a, d - 1], r1.at[a, d - 1], first_peer(a, d))
    for a in (0, 1):
        for d in (1, 3, 2):
            second[a, 0, d] = send(srcs[a], alls[a].at[here], s2.at[a, 0, d - 1], r2.at[a, 0, d - 1], second_peer(a, d))
    own = []
    for a in (0, 1):
        copy = pltpu.make_async_copy(srcs[a], alls[a].at[here], own_sem.at[a])
        copy.start()
        own.append(copy)
    lse_copy = send(lse_ref, pair_lse, ps.at[0], pr.at[0], pair)

    ones = jnp.ones((8, D), BF)
    for h in range(H):
        cols = slice(h * D, (h + 1) * D)
        prod = g_ref[:, cols].astype(F32) * o_ref[:, cols].astype(F32)
        hi = prod.astype(BF)
        lo = (prod - hi.astype(F32)).astype(BF)
        total = dot(ones, hi, 1, 1) + dot(ones, lo, 1, 1)
        delta[h : h + 1, :] = total[0:1, :]
    delta_copy = send(delta, pair_delta, ps.at[1], pr.at[1], pair)

    for s in (1, 3, 2):
        for a in (0, 1):
            first[a, s].wait_recv()
            block = alls[a].at[slot_from(a, s)]
            for d in (1, 3, 2):
                second[a, s, d] = send(block, block, s2.at[a, s, d - 1], r2.at[a, s, d - 1], second_peer(a, d))
    for copy in own:
        copy.wait()
    for copy in second.values():
        copy.wait_recv()
    for copy in (lse_copy, delta_copy):
        copy.wait()
    for copy in list(first.values()) + list(second.values()):
        copy.wait_send()


def gather(keys, values, out_grad, outputs, lse):
    return pl.pallas_call(
        gather_kernel,
        out_shape=(
            jax.ShapeDtypeStruct((PLANE, T, D), BF),
            jax.ShapeDtypeStruct((PLANE, T, D), BF),
            jax.ShapeDtypeStruct((H, T), F32),
            jax.ShapeDtypeStruct((H, T), F32),
            jax.ShapeDtypeStruct((H, T), F32),
        ),
        in_specs=[VM] * 5,
        out_specs=(VM,) * 5,
        scratch_shapes=[
            pltpu.SemaphoreType.DMA((2,)),
            pltpu.SemaphoreType.DMA((2, 3)),
            pltpu.SemaphoreType.DMA((2, 3)),
            pltpu.SemaphoreType.DMA((2, 4, 3)),
            pltpu.SemaphoreType.DMA((2, 4, 3)),
            pltpu.SemaphoreType.DMA((2,)),
            pltpu.SemaphoreType.DMA((2,)),
        ],
        compiler_params=pltpu.CompilerParams(
            collective_id=0, has_side_effects=True, vmem_limit_bytes=VMEM_LIMIT
        ),
        name="gather_kv",
    )(keys, values, out_grad, outputs, lse)


def attend_kernel(
    start, who, order, lens, q_ref, g_ref, lse_ref, delta_ref, k_ref, v_ref, *rest
):
    if start:
        dq_ref, dk, dv = rest[:3]
        scratch = rest[3:]
        dk[...] = jnp.zeros_like(dk)
        dv[...] = jnp.zeros_like(dv)
    else:
        dk_in, dv_in, dq_ref, dk_out, dv_out = rest[:5]
        scratch = rest[5:]
        dk, dv = dk_in, dv_in
    inv, ends, item_q, item_a, item_b, pos_a, pos_b, qr, gr, lr, dr, qpos, qfrom, dqa, pbuf, dbuf = scratch
    owner, plane = who[0], who[1]

    def invert(s, c):
        inv[order[s]] = s
        return c

    lax.fori_loop(0, 64, invert, 0)

    def add_end(d, c):
        c = c + lens[d]
        ends[d] = c
        return c

    lax.fori_loop(0, 16, add_end, jnp.int32(0))
    lane = lax.broadcasted_iota(I32, (1, 2 * B), 1) % B

    count = jnp.int32(0)
    for blk in (0, 1):
        at = order[owner * 2 + blk]
        base = at * B
        places = base + lane
        begin = jnp.zeros_like(places)
        low = jnp.int32(0)
        for d in range(16):
            begin = jnp.where(ends[d] <= places, ends[d], begin)
            low = jnp.where(ends[d] <= base, ends[d], low)
        qpos[blk] = places
        qfrom[blk] = begin

        def visit(p, c):
            n, half = c
            s = inv[p]
            dev = s // 2
            mine = (dev // 4) % 2 == plane
            slot = ((dev // 8) * RING + dev % 4) * 2 + s % 2

            @pl.when(mine & (half == 0))
            def _():
                item_q[n] = blk
                item_a[n] = slot
                pos_a[n] = p * B
                item_b[n] = 0
                pos_b[n] = 1 << 20

            @pl.when(mine & (half == 1))
            def _():
                item_b[n] = slot
                pos_b[n] = p * B

            full = mine & (half == 1)
            return jnp.where(full, n + 1, n), jnp.where(mine, 1 - half, half)

        n, half = lax.fori_loop(low // B, at + 1, visit, (count, jnp.int32(0)))
        count = n + half

    item_q[count] = 0
    item_a[count] = 0
    item_b[count] = 0
    pos_a[count] = 1 << 20
    pos_b[count] = 1 << 20

    for blk in (0, 1):
        rows = slice(blk * B, (blk + 1) * B)
        for h in range(H):
            cols = slice(h * D, (h + 1) * D)
            qr[blk, cols, :] = q_ref[rows, cols]
            gr[blk, cols, :] = g_ref[rows, cols]
            lr[blk, :, cols] = lse_ref[h : h + 1, rows]
            dr[blk, :, cols] = delta_ref[h : h + 1, rows]
    dqa[...] = jnp.zeros_like(dqa)
    scale = jnp.float32(D**-0.5)
    down = lax.broadcasted_iota(I32, (B, 2 * B), 0)

    def one(n, par):
        blk, a, b = item_q[n], item_a[n], item_b[n]
        kk = jnp.concatenate([k_ref[a], k_ref[b]], axis=0)
        vv = jnp.concatenate([v_ref[a], v_ref[b]], axis=0)
        key_pos = jnp.concatenate([pos_a[n] + down, pos_b[n] + down], axis=0)
        allowed = (key_pos <= qpos[blk]) & (key_pos >= qfrom[blk])
        for half in range(4):
            cols = slice(half * 256, (half + 1) * 256)
            score = dot(kk, qr[blk, cols, :], 1, 1)
            dprob = dot(vv, gr[blk, cols, :], 1, 1)
            prob = jnp.where(allowed, jnp.exp(score * scale - lr[blk, :, cols]), 0.0)
            pbuf[par, :, cols] = prob.astype(BF)
            dbuf[par, :, cols] = (prob * (dprob - dr[blk, :, cols])).astype(BF)
        dqa[blk] += dot(kk, dbuf[par], 0, 0)
        dv_term = jnp.dot(pbuf[par], gr[blk], preferred_element_type=F32)
        dk_term = jnp.dot(dbuf[par], qr[blk], preferred_element_type=F32)
        dk[a] += dk_term[:B]
        dk[b] += dk_term[B:]
        dv[a] += dv_term[:B]
        dv[b] += dv_term[B:]

    def two(i, c):
        one(2 * i, 0)
        one(2 * i + 1, 1)
        return c

    lax.fori_loop(0, (count + 1) // 2, two, 0)

    for blk in (0, 1):
        for h in range(H):
            cols = slice(h * D, (h + 1) * D)
            dq_ref[blk * B : (blk + 1) * B, cols] = dqa[blk, :, cols].T.astype(dq_ref.dtype)
    if not start:
        dk_out[...] = dk[...].astype(BF)
        dv_out[...] = dv[...].astype(BF)


def attend(who, order, lens, q, g, lse, delta, k, v, sums=None):
    start = sums is None
    kind = F32 if start else BF
    grads = jax.ShapeDtypeStruct((2 * PLANE, B, D), kind)
    args = [who, order, lens, q, g, lse, delta, k, v] + ([] if start else list(sums))
    return pl.pallas_call(
        functools.partial(attend_kernel, start),
        out_shape=(jax.ShapeDtypeStruct((T, H * D), kind), grads, grads),
        in_specs=[SM] * 3 + [VM] * (len(args) - 3),
        out_specs=(VM,) * 3,
        scratch_shapes=[
            pltpu.SMEM((64,), I32),
            pltpu.SMEM((16,), I32),
            pltpu.SMEM((72,), I32),
            pltpu.SMEM((72,), I32),
            pltpu.SMEM((72,), I32),
            pltpu.SMEM((72,), I32),
            pltpu.SMEM((72,), I32),
            pltpu.VMEM((2, H * B, D), BF),
            pltpu.VMEM((2, H * B, D), BF),
            pltpu.VMEM((2, 1, H * B), F32),
            pltpu.VMEM((2, 1, H * B), F32),
            pltpu.VMEM((2, 1, 2 * B), I32),
            pltpu.VMEM((2, 1, 2 * B), I32),
            pltpu.VMEM((2, D, H * B), F32),
            pltpu.VMEM((2, 2 * B, H * B), BF),
            pltpu.VMEM((2, 2 * B, H * B), BF),
        ],
        compiler_params=pltpu.CompilerParams(vmem_limit_bytes=VMEM_LIMIT),
        name="attend_own" if start else "attend_pair",
    )(*args)


def reduce_kernel(dk_ref, dv_ref, key_ref, value_ref, in1, out2, in2, s1, r1, s2, r2):
    z, y, x = coords()
    greet(z, y, x, False)
    srcs = (dk_ref, dv_ref)

    def send(src, dst, ssem, rsem, to):
        copy = pltpu.make_async_remote_copy(
            src_ref=src, dst_ref=dst, send_sem=ssem, recv_sem=rsem, device_id=to, device_id_type=MESH
        )
        copy.start()
        return copy

    def first_peer(a, d):
        return ident(step_of(z, d), y, x) if a == 0 else ident(z, y, step_of(x, d))

    def second_peer(a, e):
        return first_peer(1 - a, e)

    def slot(a, d, e):
        if a == 0:
            return step_of(z, d) * RING + step_of(x, e)
        return step_of(z, e) * RING + step_of(x, d)

    first, second = {}, {}
    for e in (2, 1, 3, 0):
        for a in (0, 1):
            for d in (2, 1, 3):
                first[a, e, d] = send(
                    srcs[a].at[slot(a, d, e)], in1.at[a, e, d - 1], s1.at[a, e, d - 1], r1.at[a, e, d - 1],
                    first_peer(a, d),
                )
    outs, scales = (key_ref, value_ref), (jnp.float32(D**-0.5), jnp.float32(1.0))
    sums = []
    for e in (2, 1, 3, 0):
        for a in (0, 1):
            total = srcs[a][slot(a, 0, e)].astype(F32)
            for d in (1, 2, 3):
                first[a, e, d].wait_recv()
                total = total + in1[a, e, d - 1].astype(F32)
            if e:
                out2[a, e - 1] = total.astype(BF)
                second[a, e] = send(out2.at[a, e - 1], in2.at[a, e - 1], s2.at[a, e - 1], r2.at[a, e - 1], second_peer(a, e))
            else:
                sums.append(total)
    for a in (0, 1):
        total = sums[a]
        for e in (1, 2, 3):
            second[a, e].wait_recv()
            total = total + in2[a, e - 1].astype(F32)
        outs[a][...] = (total * scales[a]).astype(BF)
    for copy in list(first.values()) + list(second.values()):
        copy.wait_send()


def reduce(dk, dv):
    grad = jax.ShapeDtypeStruct((T, D), BF)
    return pl.pallas_call(
        reduce_kernel,
        out_shape=(grad, grad),
        in_specs=[VM] * 2,
        out_specs=(VM,) * 2,
        scratch_shapes=[
            pltpu.VMEM((2, 4, 3, T, D), BF),
            pltpu.VMEM((2, 3, T, D), BF),
            pltpu.VMEM((2, 3, T, D), BF),
            pltpu.SemaphoreType.DMA((2, 4, 3)),
            pltpu.SemaphoreType.DMA((2, 4, 3)),
            pltpu.SemaphoreType.DMA((2, 3)),
            pltpu.SemaphoreType.DMA((2, 3)),
        ],
        compiler_params=pltpu.CompilerParams(
            collective_id=1, has_side_effects=True, vmem_limit_bytes=VMEM_LIMIT
        ),
        name="reduce_dkv",
    )(dk, dv)


def local(queries, keys, values, outputs, out_grad, lse, block_order, doc_lengths):
    me = lax.axis_index("ctx").astype(I32)
    plane = (me // 4) % 2
    swap = [(i, i ^ 4) for i in range(32)]
    pair_q = lax.ppermute(queries, "ctx", swap)
    pair_g = lax.ppermute(out_grad, "ctx", swap)
    ka, va, delta, pair_delta, pair_lse = gather(keys, values, out_grad, outputs, lse)
    k = ka.reshape(2 * PLANE, B, D)
    v = va.reshape(2 * PLANE, B, D)
    own = jnp.stack([me, plane])
    other = jnp.stack([me ^ 4, plane])
    dq_own, dk, dv = attend(own, block_order, doc_lengths, queries, out_grad, lse, delta, k, v)
    dq_pair, dk, dv = attend(
        other, block_order, doc_lengths, pair_q, pair_g, pair_lse, pair_delta, k, v, (dk, dv)
    )
    dq_back = lax.ppermute(dq_pair, "ctx", swap)
    key_grad, value_grad = reduce(dk.reshape(PLANE, T, D), dv.reshape(PLANE, T, D))
    query_grad = (jnp.float32(D**-0.5) * (dq_own + dq_back.astype(F32))).astype(BF)
    return (query_grad, key_grad, value_grad)


def solution(mesh):
    rows = P(("dp", "ctx"), None)
    return jax.shard_map(
        local,
        mesh=mesh,
        in_specs=(rows, rows, rows, rows, rows, P(None, ("dp", "ctx")), P("dp"), P("dp")),
        out_specs=(rows, rows, rows),
        check_vma=False,
    )
```

time: 735 us -> 93.5 us (0.13)
  the two profiles are of different devices: /device:TPU:0 before, /device:TPU:14 now
where the time goes in v1:
time: 93.5 us; the launch traced here: 93.3 us
  Pallas kernels  84 us (90%)
  starting transfers between devices  4.22 us (5%)
  local copies, waits for them, and re-layouts  2.22 us (2%)
  other arithmetic  2.12 us (2%)
    pallas_call x1, Pallas kernels, reduce(): pl.pallas_call(reduce_kernel, out_shape=(grad, grad), in_specs=[VM] * 2,...  41.7 us
    pallas_call x1, Pallas kernels, gather(): pl.pallas_call(gather_kernel, out_shape=(jax.ShapeDtypeStruct((PLANE, T,...  25.4 us
    pallas_call x2, Pallas kernels, attend(): pl.pallas_call(functools.partial(attend_kernel, start), out_shape=(jax.Sh...  16.9 us
    ppermute x1, starting transfers between devices, local(): pair_q = lax.ppermute(queries, 'ctx', swap)  2.37 us
    unnamed x12, local copies, waits for them, and re-layouts  2.22 us
  transfers between devices with their start and end apart: 3, of which 0 were waited for; matrix products, arithmetic and copies ran while one was open for 1% of the time, Pallas kernels for 82%

profile of v1, /device:TPU:14, one launch (start us, length us, event | category | flops | bytes accessed | tf_op | source)
XLA Modules:
  0.0 93.3 jit_solution(1911740201232690133)
XLA Ops:
  0.6 2.4 %collective-permute-start = (bf16[256,1024]{1,0:T(8,128)(2,1)}, bf16[256,1024]{1,0:T(8,128)(2,1)S(1)}, u32[]{:S(2)}, u32[]{:S(2)}) collective-permute-start(bf16[256,1024]{1,0:T(8,128)(2,1)} %q_ref.1), channel_id=1, source_target_pairs={{0,16},{4,20},{8,24},{12,28},{16,0},{20,4},{24,8},{28,12},{32,48},... | collective-permute-start | bytes 1572872 | tf_op jit(solution)/shard_map/ppermute | solution.py:386
  3.0 1.2 %collective-permute-start.1 = (bf16[256,1024]{1,0:T(8,128)(2,1)}, bf16[256,1024]{1,0:T(8,128)(2,1)S(1)}, u32[]{:S(2)}, u32[]{:S(2)}) collective-permute-start(bf16[256,1024]{1,0:T(8,128)(2,1)} %g_ref.3), channel_id=1, source_target_pairs={{0,16},{4,20},{8,24},{12,28},{16,0},{20,4},{24,8},{28,12},{32,48},... | collective-permute-start | bytes 1572872 | tf_op jit(solution)/shard_map/ppermute | solution.py:387
  4.2 25.4 %gather_kv.1 = (bf16[16,256,128]{2,1,0:T(8,128)(2,1)}, bf16[16,256,128]{2,1,0:T(8,128)(2,1)}, f32[8,256]{1,0:T(8,128)}, f32[8,256]{1,0:T(8,128)}, f32[8,256]{1,0:T(8,128)}) custom-call(bf16[256,128]{1,0:T(8,128)(2,1)} %k_ref.1, bf16[256,128]{1,0:T(8,128)(2,1)} %v_ref.1, bf16[256,1024]{1,0:T(8,128)(2,1)} %g_ref.3, bf16[256,1024]{1,0:T(8,128)(2,1)} %o_ref.1, ...), custom_call_target="tpu_custom_call" | custom-call | tf_op jit(solution)/shard_map/gather_kv/pallas_call | solution.py:122
  29.7 0.6 pad_add_fusion.who
  30.2 9.1 %attend_own.1 = (f32[256,1024]{1,0:T(8,128)}, f32[32,128,128]{2,1,0:T(8,128)}, f32[32,128,128]{2,1,0:T(8,128)}) custom-call(s32[2]{0:T(128)} %pad_add_fusion.who, s32[64]{0:T(128)} %order.3, s32[16]{0:T(128)} %lens.3, bf16[256,1024]{1,0:T(8,128)(2,1)} %q_ref.1, bf16[256,1024]{1,0:T(8,128)(2,1)} %g_ref.3, f32[8,256]{1,0:T(8,128)} %lse_ref.3, ...), custom_call_target="tpu_custom_call" | custom-call | tf_op jit(solution)/shard_map/attend_own/pallas_call | solution.py:277
  39.3 0.6 pad_add_fusion.1.who
  39.9 0.0 collective-permute-done.q_ref
  39.9 0.0 copy-start.1
  39.9 0.0 collective-permute-done.1.g_ref
  39.9 0.0 copy-start.2
  39.9 0.8 copy-done.1
  40.7 0.2 copy-done.2
  40.9 7.9 %attend_pair.1 = (bf16[256,1024]{1,0:T(8,128)(2,1)}, bf16[32,128,128]{2,1,0:T(8,128)(2,1)}, bf16[32,128,128]{2,1,0:T(8,128)(2,1)}) custom-call(s32[2]{0:T(128)} %pad_add_fusion.1.who, s32[64]{0:T(128)} %order.3, s32[16]{0:T(128)} %lens.3, bf16[256,1024]{1,0:T(8,128)(2,1)} %copy-done.1, bf16[256,1024]{1,0:T(8,128)(2,1)} %copy-done.2, ...), custom_call_target="tpu_custom_call" | custom-call | tf_op jit(solution)/shard_map/attend_pair/pallas_call | solution.py:277
  48.7 0.0 copy-start
  48.7 0.6 collective-permute-start.2
  49.4 41.7 %reduce_dkv.1 = (bf16[256,128]{1,0:T(8,128)(2,1)}, bf16[256,128]{1,0:T(8,128)(2,1)}) custom-call(bf16[16,256,128]{2,1,0:T(8,128)(2,1)} %bitcast.11, bf16[16,256,128]{2,1,0:T(8,128)(2,1)} %bitcast.12), custom_call_target="tpu_custom_call" | custom-call | tf_op jit(solution)/shard_map/reduce_dkv/pallas_call | solution.py:361
  91.0 0.0 copy-start.4
  91.0 0.0 copy-start.3
  91.1 0.0 collective-permute-done.2
  91.1 0.0 copy-done
  91.1 1.0 %multiply_convert_fusion = bf16[256,1024]{1,0:T(8,128)(2,1)} fusion(f32[256,1024]{1,0:T(8,128)S(1)} %copy-done, bf16[256,1024]{1,0:T(8,128)(2,1)S(1)} %collective-permute-done.2), kind=kLoop, calls=%fused_computation | loop fusion | flops 1048576 | bytes 2097152 | tf_op jit(solution)/shard_map/convert_element_type | solution.py:399
  92.0 0.0 copy-done.4
  92.0 0.6 copy.13
  92.7 0.0 copy-done.3
  92.7 0.6 copy.14
Async XLA Ops:
  0.6 39.3 %collective-permute-start = (bf16[256,1024]{1,0:T(8,128)(2,1)}, bf16[256,1024]{1,0:T(8,128)(2,1)S(1)}, u32[]{:S(2)}, u32[]{:S(2)}) collective-permute-start(bf16[256,1024]{1,0:T(8,128)(2,1)} %q_ref.1), channel_id=1, source_target_pairs={{0,16},{4,20},{8,24},{12,28},{16,0},{20,4},{24,8},{28,12},{32,48},... | collective-permute-start | bytes 1572872 | tf_op jit(solution)/shard_map/ppermute | solution.py:386
  3.0 36.9 %collective-permute-start.1 = (bf16[256,1024]{1,0:T(8,128)(2,1)}, bf16[256,1024]{1,0:T(8,128)(2,1)S(1)}, u32[]{:S(2)}, u32[]{:S(2)}) collective-permute-start(bf16[256,1024]{1,0:T(8,128)(2,1)} %g_ref.3), channel_id=1, source_target_pairs={{0,16},{4,20},{8,24},{12,28},{16,0},{20,4},{24,8},{28,12},{32,48},... | collective-permute-start | bytes 1572872 | tf_op jit(solution)/shard_map/ppermute | solution.py:387
  39.9 0.8 copy-start.1
  39.9 1.0 %copy-start.2 = (bf16[256,1024]{1,0:T(8,128)(2,1)}, bf16[256,1024]{1,0:T(8,128)(2,1)S(1)}, u32[]{:S(2)}) copy-start(bf16[256,1024]{1,0:T(8,128)(2,1)S(1)} %collective-permute-done.1.g_ref) | copy-start | bytes 1572868
  48.7 42.3 %copy-start = (f32[256,1024]{1,0:T(8,128)S(1)}, f32[256,1024]{1,0:T(8,128)}, u32[]{:S(2)}) copy-start(f32[256,1024]{1,0:T(8,128)} %get-tuple-element.19) | copy-start | bytes 3145732
  48.7 42.3 %collective-permute-start.2 = (bf16[256,1024]{1,0:T(8,128)(2,1)}, bf16[256,1024]{1,0:T(8,128)(2,1)S(1)}, u32[]{:S(2)}, u32[]{:S(2)}) collective-permute-start(bf16[256,1024]{1,0:T(8,128)(2,1)} %get-tuple-element.24), channel_id=1, source_target_pairs={{0,16},{4,20},{8,24},{12,28},{16,0},{20,4},{24,8},{28,12},{32,48},... | collective-permute-start | bytes 1572872 | tf_op jit(solution)/shard_map/ppermute | solution.py:397
  91.0 1.0 %copy-start.4 = (bf16[256,128]{1,0:T(8,128)(2,1)S(1)}, bf16[256,128]{1,0:T(8,128)(2,1)}, u32[]{:S(2)}) copy-start(bf16[256,128]{1,0:T(8,128)(2,1)} %get-tuple-element.33) | copy-start | bytes 196612
  91.0 1.6 %copy-start.3 = (bf16[256,128]{1,0:T(8,128)(2,1)S(1)}, bf16[256,128]{1,0:T(8,128)(2,1)}, u32[]{:S(2)}) copy-start(bf16[256,128]{1,0:T(8,128)(2,1)} %get-tuple-element.34) | copy-start | bytes 196612

commit v2 on v1

v2 whole, which is shorter than its diff:
```python
import jax
import jax.numpy as jnp
from jax import lax
from jax.experimental import pallas as pl
from jax.experimental.pallas import tpu as pltpu
from jax.sharding import PartitionSpec as P

BF = jnp.bfloat16
F32 = jnp.float32
I32 = jnp.int32
MESH = pl.DeviceIdType.MESH
VM = pl.BlockSpec(memory_space=pltpu.VMEM)
SM = pl.BlockSpec(memory_space=pltpu.SMEM)
ANY = pl.BlockSpec(memory_space=pl.ANY)

RING = 4
PLANE = RING * RING
T = 256
B = 128
H = 8
D = 128
VMEM_LIMIT = 32 * 2**20


def dot(a, b, ca, cb):
    return lax.dot_general(a, b, (((ca,), (cb,)), ((), ())), preferred_element_type=F32)


def stay(array):
    return pltpu.with_memory_space_constraint(array, pltpu.HBM)


def coords():
    me = lax.axis_index("ctx")
    return me // 8, (me // 4) % 2, me % 4


def ident(z, y, x):
    return {"ctx": z * 8 + y * 4 + x}


def step_of(v, d):
    return lax.rem(v + d, RING)


def greet(z, y, x, pair):
    barrier = pltpu.get_barrier_semaphore()
    others = [ident(z, y, step_of(x, d)) for d in (1, 2, 3)]
    others += [ident(step_of(z, d), y, x) for d in (1, 2, 3)]
    if pair:
        others.append(ident(z, 1 - y, x))
    for other in others:
        pl.semaphore_signal(barrier, inc=1, device_id=other, device_id_type=MESH)
    pl.semaphore_wait(barrier, len(others))


def gather_kernel(
    k_ref, v_ref, q_ref, g_ref, o_ref, lse_ref, ka, va, qa, ga, qt, gt, lses, deltas,
    outs, own_sem, s1, r1, s2, r2, ps, pr,
):
    z, y, x = coords()
    here = z * RING + x
    pair = ident(z, 1 - y, x)

    def keep(src, dst, sem):
        copy = pltpu.make_async_copy(src, dst, sem)
        copy.start()
        return copy

    grads_in = [keep(g_ref.at[pl.ds(blk * B, B)], ga.at[blk], own_sem.at[blk]) for blk in (0, 1)]
    outs_in = keep(o_ref, outs, own_sem.at[2])
    lse_in = keep(lse_ref, lses.at[0], own_sem.at[3])
    rows_in = [keep(q_ref.at[pl.ds(blk * B, B)], qa.at[blk], own_sem.at[4 + blk]) for blk in (0, 1)]
    own = [keep(src, dst.at[here], own_sem.at[6 + a]) for a, (src, dst) in enumerate(((k_ref, ka), (v_ref, va)))]
    greet(z, y, x, True)

    def send(src, dst, ssem, rsem, to):
        copy = pltpu.make_async_remote_copy(
            src_ref=src, dst_ref=dst, send_sem=ssem, recv_sem=rsem, device_id=to, device_id_type=MESH
        )
        copy.start()
        return copy

    srcs, alls = (k_ref, v_ref), (ka, va)

    def first_peer(a, d):
        return ident(z, y, step_of(x, d)) if a == 0 else ident(step_of(z, d), y, x)

    def second_peer(a, d):
        return first_peer(1 - a, d)

    def slot_from(a, s):
        return z * RING + step_of(x, RING - s) if a == 0 else step_of(z, RING - s) * RING + x

    first, second = {}, {}
    for a in (0, 1):
        for d in (1, 3, 2):
            first[a, d] = send(srcs[a], alls[a].at[here], s1.at[a, d - 1], r1.at[a, d - 1], first_peer(a, d))
    across = [send(lse_ref, lses.at[1], ps.at[4], pr.at[4], pair)]
    for blk in (0, 1):
        for i, (src, dst) in enumerate(((q_ref, qa), (g_ref, ga))):
            n = 2 * blk + i
            across.append(send(src.at[pl.ds(blk * B, B)], dst.at[2 + blk], ps.at[n], pr.at[n], pair))
    for a in (0, 1):
        for d in (1, 3, 2):
            second[a, 0, d] = send(srcs[a], alls[a].at[here], s2.at[a, 0, d - 1], r2.at[a, 0, d - 1], second_peer(a, d))
    for copy in grads_in + [outs_in]:
        copy.wait()
    ones = jnp.ones((8, D), BF)
    for h in range(H):
        cols = slice(h * D, (h + 1) * D)
        grad = jnp.concatenate([ga[0, :, cols], ga[1, :, cols]], axis=0)
        prod = grad.astype(F32) * outs[:, cols].astype(F32)
        hi = prod.astype(BF)
        lo = (prod - hi.astype(F32)).astype(BF)
        total = dot(ones, hi, 1, 1) + dot(ones, lo, 1, 1)
        deltas[0, h : h + 1, :] = total[0:1, :]
    across.append(send(deltas.at[0], deltas.at[1], ps.at[5], pr.at[5], pair))

    for s in (1, 3, 2):
        for a in (0, 1):
            first[a, s].wait_recv()
            block = alls[a].at[slot_from(a, s)]
            for d in (1, 3, 2):
                second[a, s, d] = send(block, block, s2.at[a, s, d - 1], r2.at[a, s, d - 1], second_peer(a, d))

    def turn(src, dst, blk):
        for h in range(H):
            cols = slice(h * D, (h + 1) * D)
            dst[blk, :, cols] = src[blk, :, cols].T

    for copy in own + rows_in + [lse_in]:
        copy.wait()
    for blk in (0, 1):
        turn(qa, qt, blk)
        turn(ga, gt, blk)
    for copy in second.values():
        copy.wait_recv()
    across[0].wait_recv()
    across[5].wait_recv()
    for blk in (0, 1):
        across[1 + 2 * blk].wait_recv()
        turn(qa, qt, 2 + blk)
        across[2 + 2 * blk].wait_recv()
        turn(ga, gt, 2 + blk)
    for copy in list(first.values()) + list(second.values()) + across:
        copy.wait_send()


def gather(keys, values, queries, out_grad, outputs, lse):
    dma = pltpu.SemaphoreType.DMA
    return pl.pallas_call(
        gather_kernel,
        out_shape=(
            pltpu.VMEM((PLANE, T, D), BF),
            pltpu.VMEM((PLANE, T, D), BF),
            pltpu.VMEM((4, B, H * D), BF),
            pltpu.VMEM((4, B, H * D), BF),
            pltpu.VMEM((4, D, H * B), BF),
            pltpu.VMEM((4, D, H * B), BF),
            pltpu.VMEM((2, H, T), F32),
            pltpu.VMEM((2, H, T), F32),
        ),
        in_specs=[ANY] * 6,
        out_specs=(VM,) * 8,
        scratch_shapes=[
            pltpu.VMEM((T, H * D), BF),
            dma((8,)), dma((2, 3)), dma((2, 3)), dma((2, 4, 3)), dma((2, 4, 3)), dma((6,)), dma((6,)),
        ],
        compiler_params=pltpu.CompilerParams(
            collective_id=0, has_side_effects=True, vmem_limit_bytes=VMEM_LIMIT
        ),
        name="gather_rows",
    )(*[stay(t) for t in (keys, values, queries, out_grad, outputs, lse)])


def attend_kernel(
    order, lens, qa, ga, qt, gt, lse_ref, delta_ref, k_ref, v_ref, dq_own, dq_pair, dk_out, dv_out,
    inv, ends, item_q, item_a, item_b, pos_a, pos_b, lc, dc, qfrom, qbase, dqa, dk, dv, pbuf, dbuf,
):
    me = lax.axis_index("ctx")
    plane = (me // 4) % 2
    mate = me + 4 - 8 * plane
    dk[...] = jnp.zeros_like(dk)
    dv[...] = jnp.zeros_like(dv)

    def invert(s, c):
        inv[order[s]] = s
        return c

    lax.fori_loop(0, 64, invert, 0)

    def add_end(d, c):
        c = c + lens[d]
        ends[d] = c
        return c

    lax.fori_loop(0, 16, add_end, jnp.int32(0))
    row = lax.broadcasted_iota(I32, (B, D), 0)

    count = jnp.int32(0)
    for blk in range(4):
        at = order[(me, mate)[blk // 2] * 2 + blk % 2]
        base = at * B
        places = base + row
        begin = jnp.zeros_like(places)
        low = jnp.int32(0)
        for d in range(16):
            begin = jnp.where(ends[d] <= places, ends[d], begin)
            low = jnp.where(ends[d] <= base, ends[d], low)
        qfrom[blk] = begin
        qbase[blk] = base

        def visit(p, c):
            n, half = c
            s = inv[p]
            dev = s // 2
            mine = (dev // 4) % 2 == plane
            slot = ((dev // 8) * RING + dev % 4) * 2 + s % 2

            @pl.when(mine & (half == 0))
            def _():
                item_q[n] = blk
                item_a[n] = slot
                pos_a[n] = p * B
                item_b[n] = 0
                pos_b[n] = 1 << 20

            @pl.when(mine & (half == 1))
            def _():
                item_b[n] = slot
                pos_b[n] = p * B

            full = mine & (half == 1)
            return jnp.where(full, n + 1, n), jnp.where(mine, 1 - half, half)

        n, half = lax.fori_loop(low // B, at + 1, visit, (count, jnp.int32(0)))
        count = n + half

    item_q[count] = 0
    item_a[count] = 0
    item_b[count] = 0
    pos_a[count] = 1 << 20
    pos_b[count] = 1 << 20

    head_of = lax.broadcasted_iota(I32, (3 * H, D), 0) % H

    def pieces(ref, side, rows):
        whole = jnp.minimum(ref[side, :, rows], 1e30)
        hi = whole.astype(BF)
        left = whole - hi.astype(F32)
        mid = left.astype(BF)
        lo = (left - mid.astype(F32)).astype(BF)
        return jnp.concatenate([hi.astype(F32), mid.astype(F32), lo.astype(F32)], axis=0).astype(BF)

    for blk in range(4):
        rows = slice(blk % 2 * B, (blk % 2 + 1) * B)
        lse_parts = pieces(lse_ref, blk // 2, rows)
        delta_parts = pieces(delta_ref, blk // 2, rows)
        for h in range(H):
            cols = slice(h * D, (h + 1) * D)
            select = jnp.where(head_of == h, 1.0, 0.0).astype(BF)
            lc[blk, cols, :] = dot(lse_parts, select, 0, 0)
            dc[blk, cols, :] = dot(delta_parts, select, 0, 0)
    dqa[...] = jnp.zeros_like(dqa)
    scale = jnp.float32(D**-0.5)
    across = lax.broadcasted_iota(I32, (1, B), 1)

    def load(n):
        a, b = item_a[n], item_b[n]
        return (
            jnp.concatenate([k_ref[a], k_ref[b]], axis=0),
            jnp.concatenate([v_ref[a], v_ref[b]], axis=0),
        )

    def scores(n, par, kk, vv):
        blk = item_q[n]
        key_pos = jnp.concatenate([pos_a[n] + across, pos_b[n] + across], axis=1)
        here = qbase[blk] + row
        here = jnp.concatenate([here, here], axis=1)
        begin = qfrom[blk]
        begin = jnp.concatenate([begin, begin], axis=1)
        allowed = (key_pos <= here) & (key_pos >= begin)
        allowed = jnp.concatenate([allowed, allowed], axis=0)
        for two in range(4):
            cols = slice(two * 256, (two + 1) * 256)
            heads = [slice((2 * two + i) * D, (2 * two + i + 1) * D) for i in (0, 1)]
            score = dot(jnp.concatenate([qa[blk, :, c] for c in heads], axis=0), kk, 1, 1)
            dprob = dot(jnp.concatenate([ga[blk, :, c] for c in heads], axis=0), vv, 1, 1)
            less = lc[blk, cols, :]
            delta = dc[blk, cols, :]
            prob = jnp.where(allowed, jnp.exp(score * scale - jnp.concatenate([less, less], axis=1)), 0.0)
            pbuf[par, cols, :] = prob.astype(BF)
            dbuf[par, cols, :] = (prob * (dprob - jnp.concatenate([delta, delta], axis=1))).astype(BF)

    def grads(n, par, kk):
        blk, a, b = item_q[n], item_a[n], item_b[n]
        dqa[blk] += jnp.dot(dbuf[par], kk, preferred_element_type=F32)
        dv_term = jnp.dot(gt[blk], pbuf[par], preferred_element_type=F32)
        dk_term = jnp.dot(qt[blk], dbuf[par], preferred_element_type=F32)
        dk[a] += dk_term[:, :B]
        dk[b] += dk_term[:, B:]
        dv[a] += dv_term[:, :B]
        dv[b] += dv_term[:, B:]

    def two(i, c):
        k0, v0 = load(2 * i)
        k1, v1 = load(2 * i + 1)
        scores(2 * i, 0, k0, v0)
        scores(2 * i + 1, 1, k1, v1)
        grads(2 * i, 0, k0)
        grads(2 * i + 1, 1, k1)
        return c

    lax.fori_loop(0, (count + 1) // 2, two, 0)

    for blk in range(4):
        dst = (dq_own, dq_pair)[blk // 2]
        for h in range(H):
            cols = slice(h * D, (h + 1) * D)
            dst[blk % 2, :, cols] = dqa[blk, cols, :].astype(dst.dtype)
    dk_out[...] = dk[...].astype(BF)
    dv_out[...] = dv[...].astype(BF)


def attend(order, lens, *arrays):
    return pl.pallas_call(
        attend_kernel,
        out_shape=(
            pltpu.VMEM((2, B, H * D), F32),
            pltpu.VMEM((2, B, H * D), BF),
            pltpu.VMEM((2 * PLANE, D, B), BF),
            pltpu.VMEM((2 * PLANE, D, B), BF),
        ),
        in_specs=[SM] * 2 + [VM] * 8,
        out_specs=(VM,) * 4,
        scratch_shapes=[
            pltpu.SMEM((64,), I32),
            pltpu.SMEM((16,), I32),
            pltpu.SMEM((80,), I32),
            pltpu.SMEM((80,), I32),
            pltpu.SMEM((80,), I32),
            pltpu.SMEM((80,), I32),
            pltpu.SMEM((80,), I32),
            pltpu.VMEM((4, H * B, D), F32),
            pltpu.VMEM((4, H * B, D), F32),
            pltpu.VMEM((4, B, D), I32),
            pltpu.SMEM((4,), I32),
            pltpu.VMEM((4, H * B, D), F32),
            pltpu.VMEM((2 * PLANE, D, B), F32),
            pltpu.VMEM((2 * PLANE, D, B), F32),
            pltpu.VMEM((2, H * B, 2 * B), BF),
            pltpu.VMEM((2, H * B, 2 * B), BF),
        ],
        compiler_params=pltpu.CompilerParams(vmem_limit_bytes=VMEM_LIMIT),
        name="attend",
    )(stay(order), stay(lens), *arrays)


def reduce_kernel(dq_ref, dk_ref, dv_ref, back, k_sum, v_sum, in1, out2, in2, s1, r1, s2, r2, ps, pr):
    z, y, x = coords()
    greet(z, y, x, True)
    srcs = (dk_ref, dv_ref)

    def send(src, dst, ssem, rsem, to):
        copy = pltpu.make_async_remote_copy(
            src_ref=src, dst_ref=dst, send_sem=ssem, recv_sem=rsem, device_id=to, device_id_type=MESH
        )
        copy.start()
        return copy

    def first_peer(a, d):
        return ident(step_of(z, d), y, x) if a == 0 else ident(z, y, step_of(x, d))

    def second_peer(a, e):
        return first_peer(1 - a, e)

    def slot(a, d, e):
        if a == 0:
            return step_of(z, d) * RING + step_of(x, e)
        return step_of(z, e) * RING + step_of(x, d)

    first, second = {}, {}
    for e in (2, 1, 3, 0):
        for a in (0, 1):
            for d in (2, 1, 3):
                first[a, e, d] = send(
                    srcs[a].at[slot(a, d, e)], in1.at[a, e, d - 1], s1.at[a, e, d - 1], r1.at[a, e, d - 1],
                    first_peer(a, d),
                )
    across = send(dq_ref, back, ps, pr, ident(z, 1 - y, x))
    sums = []
    for e in (2, 1, 3, 0):
        for a in (0, 1):
            total = srcs[a][slot(a, 0, e)].astype(F32)
            for d in (1, 2, 3):
                first[a, e, d].wait_recv()
                total = total + in1[a, e, d - 1].astype(F32)
            if e:
                out2[a, e - 1] = total.astype(BF)
                second[a, e] = send(out2.at[a, e - 1], in2.at[a, e - 1], s2.at[a, e - 1], r2.at[a, e - 1], second_peer(a, e))
            else:
                sums.append(total)
    for a, dst in ((0, k_sum), (1, v_sum)):
        total = sums[a]
        for e in (1, 2, 3):
            second[a, e].wait_recv()
            total = total + in2[a, e - 1].astype(F32)
        dst[...] = total
    across.wait()
    for copy in list(first.values()) + list(second.values()):
        copy.wait_send()


def reduce(dq, dk, dv):
    dma = pltpu.SemaphoreType.DMA
    return pl.pallas_call(
        reduce_kernel,
        out_shape=(
            pltpu.VMEM((2, B, H * D), BF),
            pltpu.VMEM((2, D, B), F32),
            pltpu.VMEM((2, D, B), F32),
        ),
        in_specs=[VM] * 3,
        out_specs=(VM,) * 3,
        scratch_shapes=[
            pltpu.VMEM((2, 4, 3, 2, D, B), BF),
            pltpu.VMEM((2, 3, 2, D, B), BF),
            pltpu.VMEM((2, 3, 2, D, B), BF),
            dma((2, 4, 3)), dma((2, 4, 3)), dma((2, 3)), dma((2, 3)), dma, dma,
        ],
        compiler_params=pltpu.CompilerParams(
            collective_id=1, has_side_effects=True, vmem_limit_bytes=VMEM_LIMIT
        ),
        name="reduce_rows",
    )(dq, dk.reshape(PLANE, 2, D, B), dv.reshape(PLANE, 2, D, B))


def finish_kernel(dq_own, back, k_sum, v_sum, query_ref, key_ref, value_ref):
    scale = jnp.float32(D**-0.5)
    for blk in (0, 1):
        rows = slice(blk * B, (blk + 1) * B)
        query_ref[rows, :] = (scale * (dq_own[blk] + back[blk].astype(F32))).astype(BF)
        key_ref[rows, :] = (scale * k_sum[blk]).T.astype(BF)
        value_ref[rows, :] = v_sum[blk].T.astype(BF)


def finish(*arrays):
    grad = jax.ShapeDtypeStruct((T, D), BF)
    return pl.pallas_call(
        finish_kernel,
        out_shape=(jax.ShapeDtypeStruct((T, H * D), BF), grad, grad),
        in_specs=[VM] * 4,
        out_specs=(VM,) * 3,
        compiler_params=pltpu.CompilerParams(vmem_limit_bytes=VMEM_LIMIT),
        name="finish",
    )(*arrays)


def local(queries, keys, values, outputs, out_grad, lse, block_order, doc_lengths):
    ka, va, qa, ga, qt, gt, lses, deltas = gather(keys, values, queries, out_grad, outputs, lse)
    k = ka.reshape(2 * PLANE, B, D)
    v = va.reshape(2 * PLANE, B, D)
    dq_own, dq_pair, dk, dv = attend(block_order, doc_lengths, qa, ga, qt, gt, lses, deltas, k, v)
    back, k_sum, v_sum = reduce(dq_pair, dk, dv)
    return finish(dq_own, back, k_sum, v_sum)


def solution(mesh):
    rows = P(("dp", "ctx"), None)
    return jax.shard_map(
        local,
        mesh=mesh,
        in_specs=(rows, rows, rows, rows, rows, P(None, ("dp", "ctx")), P("dp"), P("dp")),
        out_specs=(rows, rows, rows),
        check_vma=False,
    )
```

time: 93.5 us -> 75 us (0.80)
  the two profiles are of different devices: /device:TPU:14 before, /device:TPU:0 now
where the time goes in v2:
time: 75 us; the launch traced here: 74.8 us
  Pallas kernels  74.2 us (99%)
    pallas_call x1, Pallas kernels, reduce(): pl.pallas_call(reduce_kernel, out_shape=(pltpu.VMEM((2, B, H * D), BF), p...  32.8 us
    pallas_call x1, Pallas kernels, gather(): pl.pallas_call(gather_kernel, out_shape=(pltpu.VMEM((PLANE, T, D), BF), p...  32.2 us
    pallas_call x1, Pallas kernels, attend(): pl.pallas_call(attend_kernel, out_shape=(pltpu.VMEM((2, B, H * D), F32),...  8.21 us

profile of v2, /device:TPU:0, one launch (start us, length us, event | category | flops | bytes accessed | tf_op | source)
XLA Modules:
  0.0 74.8 jit_solution(6458983331947131559)
XLA Ops:
  0.6 32.2 %gather_rows.1 = (bf16[16,256,128]{2,1,0:T(8,128)(2,1)S(1)}, bf16[16,256,128]{2,1,0:T(8,128)(2,1)S(1)}, bf16[4,128,1024]{2,1,0:T(8,128)(2,1)S(1)}, bf16[4,128,10...) custom-call(bf16[256,128]{1,0:T(8,128)(2,1)} %k_ref.1, ...), custom_call_target="tpu_custom_call" | custom-call | tf_op jit(solution)/shard_map/gather_rows/pallas_call | solution.py:152
  32.8 8.2 %attend.1 = (f32[2,128,1024]{2,1,0:T(8,128)S(1)}, bf16[2,128,1024]{2,1,0:T(8,128)(2,1)S(1)}, bf16[32,128,128]{2,1,0:T(8,128)(2,1)S(1)}, bf16[32,128,128]{2,1,0:T(8,128)(2,1)S(1)}) custom-call(s32[64]{0:T(128)} %order.1, s32[16]{0:T(128)} %lens.1, bf16[4,128,1024]{2,1,0:T(8,128)(2,1)S(1)} %get-tuple-element.18.qa, ...), custom_call_target="tpu_custom_call" | custom-call | tf_op jit(solution)/shard_map/attend/pallas_call | solution.py:327
  41.0 32.8 %reduce_rows.1 = (bf16[2,128,1024]{2,1,0:T(8,128)(2,1)S(1)}, f32[2,128,128]{2,1,0:T(8,128)S(1)}, f32[2,128,128]{2,1,0:T(8,128)S(1)}) custom-call(bf16[2,128,1024]{2,1,0:T(8,128)(2,1)S(1)} %get-tuple-element.27.dq_ref, bf16[16,2,128,128]{3,2,1,0:T(8,128)(2,1)S(1)} %bitcast.4, bf16[16,2,128,128]{3,2,1,0:T(8,128)(2,1)S(1)} %bitcast.5), custom_call_target="tpu_custom_call" | custom-call | tf_op jit(solution)/shard_map/reduce_rows/pallas_call | solution.py:417
  73.8 1.1 %finish.1 = (bf16[256,1024]{1,0:T(8,128)(2,1)}, bf16[256,128]{1,0:T(8,128)(2,1)}, bf16[256,128]{1,0:T(8,128)(2,1)}) custom-call(f32[2,128,1024]{2,1,0:T(8,128)S(1)} %get-tuple-element.26.dq_own, bf16[2,128,1024]{2,1,0:T(8,128)(2,1)S(1)} %get-tuple-element.30.back, f32[2,128,128]{2,1,0:T(8,128)S(1)} %get-tuple-element.31.k_sum, ...), custom_call_target="tpu_custom_call" | custom-call | tf_op jit(solution)/shard_map/finish/pallas_call | solution.py:450

commit v3 on v2

v3 whole, which is shorter than its diff:
```python
import functools

import jax
import jax.numpy as jnp
from jax import lax
from jax.experimental import pallas as pl
from jax.experimental.pallas import tpu as pltpu
from jax.sharding import PartitionSpec as P

BF = jnp.bfloat16
F32 = jnp.float32
I32 = jnp.int32
MESH = pl.DeviceIdType.MESH
VM = pl.BlockSpec(memory_space=pltpu.VMEM)
SM = pl.BlockSpec(memory_space=pltpu.SMEM)
ANY = pl.BlockSpec(memory_space=pl.ANY)

RING = 4
PLANE = RING * RING
T = 256
B = 128
H = 8
D = 128
VMEM_LIMIT = 32 * 2**20


def dot(a, b, ca, cb):
    return lax.dot_general(a, b, (((ca,), (cb,)), ((), ())), preferred_element_type=F32)


def stay(array):
    return pltpu.with_memory_space_constraint(array, pltpu.HBM)


def coords():
    me = lax.axis_index("ctx")
    return me // 8, (me // 4) % 2, me % 4


def ident(z, y, x):
    return {"ctx": z * 8 + y * 4 + x}


def step_of(v, d):
    return lax.rem(v + d, RING)


def greet_signal(z, y, x):
    barrier = pltpu.get_barrier_semaphore()
    others = [ident(z, y, step_of(x, d)) for d in (1, 2, 3)]
    others += [ident(step_of(z, d), y, x) for d in (1, 2, 3)]
    others.append(ident(z, 1 - y, x))
    for other in others:
        pl.semaphore_signal(barrier, inc=1, device_id=other, device_id_type=MESH)


def greet_wait():
    pl.semaphore_wait(pltpu.get_barrier_semaphore(), 7)


def widen(ref, dst):
    head_of = lax.broadcasted_iota(I32, (3 * H, D), 0) % H
    for blk in (0, 1):
        whole = jnp.minimum(ref[:, blk * B : (blk + 1) * B], 1e30)
        hi = whole.astype(BF)
        left = whole - hi.astype(F32)
        mid = left.astype(BF)
        lo = (left - mid.astype(F32)).astype(BF)
        parts = jnp.concatenate([hi.astype(F32), mid.astype(F32), lo.astype(F32)], axis=0).astype(BF)
        for h in range(H):
            select = jnp.where(head_of == h, 1.0, 0.0).astype(BF)
            dst[blk, h * D : (h + 1) * D, :] = dot(parts, select, 0, 0)


def gather_kernel(
    k_ref, v_ref, q_ref, g_ref, o_ref, lse_ref, ka, va, qa, ga, qt, gt, lc, dc, delta,
    outs, lses, own_sem, s1, r1, s2, r2, s3, r3,
):
    z, y, x = coords()
    here = z * RING + x

    def keep(src, dst, sem):
        copy = pltpu.make_async_copy(src, dst, sem)
        copy.start()
        return copy

    grads_in = [keep(g_ref.at[pl.ds(blk * B, B)], ga.at[blk], own_sem.at[blk]) for blk in (0, 1)]
    outs_in = keep(o_ref, outs, own_sem.at[2])
    lse_in = keep(lse_ref, lses, own_sem.at[3])
    rows_in = [keep(q_ref.at[pl.ds(blk * B, B)], qa.at[blk], own_sem.at[4 + blk]) for blk in (0, 1)]
    own = [keep(src, dst.at[here], own_sem.at[6 + a]) for a, (src, dst) in enumerate(((k_ref, ka), (v_ref, va)))]
    greet_signal(z, y, x)
    greet_wait()

    def send(src, dst, ssem, rsem, to):
        copy = pltpu.make_async_remote_copy(
            src_ref=src, dst_ref=dst, send_sem=ssem, recv_sem=rsem, device_id=to, device_id_type=MESH
        )
        copy.start()
        return copy

    srcs, alls = (k_ref, v_ref), (ka, va)

    def first_peer(a, d):
        return ident(z, y, step_of(x, d)) if a == 0 else ident(step_of(z, d), y, x)

    def second_peer(a, d):
        return first_peer(1 - a, d)

    def slot_from(a, s, t=0):
        if a == 0:
            return step_of(z, RING - t) * RING + step_of(x, RING - s)
        return step_of(z, RING - s) * RING + step_of(x, RING - t)

    first, second, third = {}, {}, {}

    def spread(a, s):
        src = srcs[a] if s == 0 else alls[a].at[slot_from(a, s)]
        dst = alls[a].at[here if s == 0 else slot_from(a, s)]
        for e in (1, 3):
            second[a, s, e] = send(src, dst, s2.at[a, s, e - 1], r2.at[a, s, e - 1], second_peer(a, e))

    for d in (1, 3, 2):
        for a in (0, 1):
            first[a, d] = send(srcs[a], alls[a].at[here], s1.at[a, d - 1], r1.at[a, d - 1], first_peer(a, d))
    for a in (0, 1):
        spread(a, 0)

    for s in (1, 3, 2):
        for a in (0, 1):
            first[a, s].wait_recv()
            spread(a, s)

    for copy in grads_in + [outs_in]:
        copy.wait()
    ones = jnp.ones((8, D), BF)
    for h in range(H):
        cols = slice(h * D, (h + 1) * D)
        grad = jnp.concatenate([ga[0, :, cols], ga[1, :, cols]], axis=0)
        prod = grad.astype(F32) * outs[:, cols].astype(F32)
        hi = prod.astype(BF)
        lo = (prod - hi.astype(F32)).astype(BF)
        total = dot(ones, hi, 1, 1) + dot(ones, lo, 1, 1)
        delta[h : h + 1, :] = total[0:1, :]

    def relay(s):
        for e, half in ((1, 0), (3, 1)):
            for a in (0, 1):
                second[a, s, e].wait_recv()
                part = alls[a].at[slot_from(a, s, e), pl.ds(half * B, B)]
                third[a, s, half] = send(part, part, s3.at[a, s, half], r3.at[a, s, half], second_peer(a, e))

    def turn(src, dst, blk):
        for h in range(H):
            cols = slice(h * D, (h + 1) * D)
            dst[blk, :, cols] = src[blk, :, cols].T

    relay(0)
    for copy in rows_in + own:
        copy.wait()
    turn(qa, qt, 0)
    turn(ga, gt, 0)
    relay(1)
    turn(qa, qt, 1)
    turn(ga, gt, 1)
    relay(3)
    lse_in.wait()
    widen(lses, lc)
    widen(delta, dc)
    relay(2)
    for copy in third.values():
        copy.wait_recv()
    for copy in list(first.values()) + list(second.values()) + list(third.values()):
        copy.wait_send()


def gather(keys, values, queries, out_grad, outputs, lse):
    dma = pltpu.SemaphoreType.DMA
    return pl.pallas_call(
        gather_kernel,
        out_shape=(
            pltpu.VMEM((PLANE, T, D), BF),
            pltpu.VMEM((PLANE, T, D), BF),
            pltpu.VMEM((2, B, H * D), BF),
            pltpu.VMEM((2, B, H * D), BF),
            pltpu.VMEM((2, D, H * B), BF),
            pltpu.VMEM((2, D, H * B), BF),
            pltpu.VMEM((2, H * B, D), F32),
            pltpu.VMEM((2, H * B, D), F32),
            pltpu.VMEM((H, T), F32),
        ),
        in_specs=[ANY] * 6,
        out_specs=(VM,) * 9,
        scratch_shapes=[
            pltpu.VMEM((T, H * D), BF),
            pltpu.VMEM((H, T), F32),
            dma((8,)), dma((2, 3)), dma((2, 3)), dma((2, 4, 3)), dma((2, 4, 3)),
            dma((2, 4, 2)), dma((2, 4, 2)),
        ],
        compiler_params=pltpu.CompilerParams(
            collective_id=0, has_side_effects=True, vmem_limit_bytes=VMEM_LIMIT
        ),
        name="gather_rows",
    )(*[stay(t) for t in (keys, values, queries, out_grad, outputs, lse)])


KEYS = 36
NEVER = 1 << 20


def attend_kernel(own, order, lens, *refs):
    if own:
        qa, ga, qt, gt, lc, dc, k_ref, v_ref, dqa, dk, dv = refs[:11]
        slots, places, qfrom, qbase, pbuf, dbuf = refs[11:]
    else:
        q_hbm, g_hbm, lse_ref, delta_ref, k_ref, v_ref, _, _, dq_out, dk, dv = refs[:11]
        slots, places, qfrom, qbase, pbuf, dbuf, qa, ga, qt, gt, lc, dc, dqa, sems = refs[11:]
        loads = []
        for blk in (0, 1):
            for i, (src, dst) in enumerate(((q_hbm, qa), (g_hbm, ga))):
                copy = pltpu.make_async_copy(src.at[pl.ds(blk * B, B)], dst.at[blk], sems.at[2 * blk + i])
                copy.start()
                loads.append(copy)
    me = lax.axis_index("ctx")
    plane = (me // 4) % 2
    owner = me if own else me + 4 - 8 * plane

    ats = [order[owner * 2 + blk] for blk in (0, 1)]
    row = lax.broadcasted_iota(I32, (B, D), 0)
    lows = [jnp.int32(0), jnp.int32(0)]
    begins = [jnp.zeros_like(row), jnp.zeros_like(row)]
    end = jnp.int32(0)
    for d in range(lens.shape[0]):
        end = end + lens[d]
        for blk in (0, 1):
            lows[blk] = jnp.where(end <= ats[blk] * B, end, lows[blk])
            begins[blk] = jnp.where(end <= ats[blk] * B + row, end, begins[blk])
    lows = [low // B for low in lows]
    for blk in (0, 1):
        qfrom[blk] = begins[blk]
        qbase[blk] = ats[blk] * B

    def list_keys(i, counts):
        counts = list(counts)
        for j in range(8):
            slot = i * 8 + j
            p = order[i * 16 + plane * 8 + j]
            for blk in (0, 1):
                slots[blk * KEYS + counts[blk]] = slot
                places[blk * KEYS + counts[blk]] = p * B
                needed = (p >= lows[blk]) & (p <= ats[blk])
                counts[blk] = counts[blk] + needed.astype(I32)
        return tuple(counts)

    counts = lax.fori_loop(0, 4, list_keys, (jnp.int32(0), jnp.int32(0)))
    for blk in (0, 1):
        for i in range(3):
            slots[blk * KEYS + counts[blk] + i] = 0
            places[blk * KEYS + counts[blk] + i] = NEVER
    items = [(count + 1) // 2 for count in counts]
    total = items[0] + items[1]

    dqa[...] = jnp.zeros_like(dqa)
    if own:
        dk[...] = jnp.zeros_like(dk)
        dv[...] = jnp.zeros_like(dv)
    else:
        widen(lse_ref, lc)
        widen(delta_ref, dc)
        for blk in (0, 1):
            for src, dst, copy in ((qa, qt, loads[2 * blk]), (ga, gt, loads[2 * blk + 1])):
                copy.wait()
                for h in range(H):
                    cols = slice(h * D, (h + 1) * D)
                    dst[blk, :, cols] = src[blk, :, cols].T
    scale = jnp.float32(D**-0.5)
    across = lax.broadcasted_iota(I32, (1, B), 1)

    def load(n):
        later = (n >= items[0]).astype(I32)
        at = later * (KEYS - 2 * items[0]) + 2 * n
        a, b = slots[at], slots[at + 1]
        kk = jnp.concatenate([k_ref[a], k_ref[b]], axis=0)
        vv = jnp.concatenate([v_ref[a], v_ref[b]], axis=0)
        return later, a, b, kk, vv, places[at], places[at + 1]

    def scores(item, par):
        blk, _, _, kk, vv, place_a, place_b = item
        key_pos = jnp.concatenate([place_a + across, place_b + across], axis=1)
        here = qbase[blk] + row
        here = jnp.concatenate([here, here], axis=1)
        begin = qfrom[blk]
        begin = jnp.concatenate([begin, begin], axis=1)
        allowed = (key_pos <= here) & (key_pos >= begin)
        allowed = jnp.concatenate([allowed, allowed], axis=0)
        for two in range(4):
            cols = slice(two * 256, (two + 1) * 256)
            heads = [slice((2 * two + i) * D, (2 * two + i + 1) * D) for i in (0, 1)]
            score = dot(jnp.concatenate([qa[blk, :, c] for c in heads], axis=0), kk, 1, 1)
            dprob = dot(jnp.concatenate([ga[blk, :, c] for c in heads], axis=0), vv, 1, 1)
            less = lc[blk, cols, :]
            delta = dc[blk, cols, :]
            prob = jnp.where(allowed, jnp.exp(score * scale - jnp.concatenate([less, less], axis=1)), 0.0)
            pbuf[par, cols, :] = prob.astype(BF)
            dbuf[par, cols, :] = (prob * (dprob - jnp.concatenate([delta, delta], axis=1))).astype(BF)

    def grads(item, par):
        blk, a, b, kk = item[:4]
        dqa[blk] += jnp.dot(dbuf[par], kk, preferred_element_type=F32)
        dv_term = jnp.dot(gt[blk], pbuf[par], preferred_element_type=F32)
        dk_term = jnp.dot(qt[blk], dbuf[par], preferred_element_type=F32)
        dk[a] += dk_term[:, :B]
        dk[b] += dk_term[:, B:]
        dv[a] += dv_term[:, :B]
        dv[b] += dv_term[:, B:]

    def two(i, c):
        now = [load(2 * i), load(2 * i + 1)]
        for par in (0, 1):
            scores(now[par], par)
        for par in (0, 1):
            grads(now[par], par)
        return c

    lax.fori_loop(0, (total + 1) // 2, two, 0)
    if not own:
        dq_out[...] = dqa[...].astype(BF)


def attend(own, order, lens, *arrays):
    sums = pltpu.VMEM((2 * PLANE, D, B), F32)
    rows = pltpu.VMEM((2, B, H * D), BF)
    cols = pltpu.VMEM((2, D, H * B), BF)
    scratch = [
        pltpu.SMEM((2 * KEYS,), I32),
        pltpu.SMEM((2 * KEYS,), I32),
        pltpu.VMEM((2, B, D), I32),
        pltpu.SMEM((2,), I32),
        pltpu.VMEM((2, H * B, 2 * B), BF),
        pltpu.VMEM((2, H * B, 2 * B), BF),
    ]
    if own:
        specs = [SM] * 2 + [VM] * 8
    else:
        specs = [SM] * 2 + [ANY] * 2 + [VM] * 6
        scratch += [rows, rows, cols, cols] + [pltpu.VMEM((2, H * B, D), F32)] * 3 + [pltpu.SemaphoreType.DMA((4,))]
        arrays = [stay(t) for t in arrays[:2]] + list(arrays[2:])
    return pl.pallas_call(
        functools.partial(attend_kernel, own),
        out_shape=(pltpu.VMEM((2, H * B, D), F32 if own else BF), sums, sums),
        in_specs=specs,
        out_specs=(VM,) * 3,
        scratch_shapes=scratch,
        input_output_aliases={} if own else {8: 1, 9: 2},
        compiler_params=pltpu.CompilerParams(vmem_limit_bytes=VMEM_LIMIT),
        name="attend_own" if own else "attend_pair",
    )(stay(order), stay(lens), *arrays)


def reduce_kernel(dq_ref, dk_ref, dv_ref, back, k_sum, v_sum, out1, in1, out2, in2, s1, r1, s2, r2, ps, pr):
    z, y, x = coords()
    greet_signal(z, y, x)
    srcs = (dk_ref, dv_ref)
    for a in (0, 1):
        out1[a] = srcs[a][...].astype(BF)
    greet_wait()

    def send(src, dst, ssem, rsem, to):
        copy = pltpu.make_async_remote_copy(
            src_ref=src, dst_ref=dst, send_sem=ssem, recv_sem=rsem, device_id=to, device_id_type=MESH
        )
        copy.start()
        return copy

    def first_peer(a, d):
        return ident(step_of(z, d), y, x) if a == 0 else ident(z, y, step_of(x, d))

    def second_peer(a, e):
        return first_peer(1 - a, e)

    def slot(a, d, e):
        if a == 0:
            return step_of(z, d) * RING + step_of(x, e)
        return step_of(z, e) * RING + step_of(x, d)

    first, second = {}, {}
    for e in (2, 1, 3, 0):
        for a in (0, 1):
            for d in (2, 1, 3):
                first[a, e, d] = send(
                    out1.at[a, slot(a, d, e)], in1.at[a, e, d - 1], s1.at[a, e, d - 1], r1.at[a, e, d - 1],
                    first_peer(a, d),
                )
    across = send(dq_ref, back, ps, pr, ident(z, 1 - y, x))
    sums = []
    for e in (2, 1, 3, 0):
        for a in (0, 1):
            total = srcs[a][slot(a, 0, e)]
            for d in (1, 2, 3):
                first[a, e, d].wait_recv()
                total = total + in1[a, e, d - 1].astype(F32)
            if e:
                out2[a, e - 1] = total.astype(BF)
                second[a, e] = send(out2.at[a, e - 1], in2.at[a, e - 1], s2.at[a, e - 1], r2.at[a, e - 1], second_peer(a, e))
            else:
                sums.append(total)
    for a, dst in ((0, k_sum), (1, v_sum)):
        total = sums[a]
        for e in (1, 2, 3):
            second[a, e].wait_recv()
            total = total + in2[a, e - 1].astype(F32)
        dst[...] = total
    across.wait()
    for copy in list(first.values()) + list(second.values()):
        copy.wait_send()


def reduce(dq, dk, dv):
    dma = pltpu.SemaphoreType.DMA
    return pl.pallas_call(
        reduce_kernel,
        out_shape=(
            pltpu.VMEM((2, H * B, D), BF),
            pltpu.VMEM((2, D, B), F32),
            pltpu.VMEM((2, D, B), F32),
        ),
        in_specs=[VM] * 3,
        out_specs=(VM,) * 3,
        scratch_shapes=[
            pltpu.VMEM((2, PLANE, 2, D, B), BF),
            pltpu.VMEM((2, 4, 3, 2, D, B), BF),
            pltpu.VMEM((2, 3, 2, D, B), BF),
            pltpu.VMEM((2, 3, 2, D, B), BF),
            dma((2, 4, 3)), dma((2, 4, 3)), dma((2, 3)), dma((2, 3)), dma, dma,
        ],
        compiler_params=pltpu.CompilerParams(
            collective_id=1, has_side_effects=True, vmem_limit_bytes=VMEM_LIMIT
        ),
        name="reduce_rows",
    )(dq, dk.reshape(PLANE, 2, D, B), dv.reshape(PLANE, 2, D, B))


def finish_kernel(dq_own, back, k_sum, v_sum, query_ref, key_ref, value_ref):
    scale = jnp.float32(D**-0.5)
    for blk in (0, 1):
        rows = slice(blk * B, (blk + 1) * B)
        for h in range(H):
            cols = slice(h * D, (h + 1) * D)
            query_ref[rows, cols] = (scale * (dq_own[blk, cols, :] + back[blk, cols, :].astype(F32))).astype(BF)
        key_ref[rows, :] = (scale * k_sum[blk]).T.astype(BF)
        value_ref[rows, :] = v_sum[blk].T.astype(BF)


def finish(*arrays):
    grad = jax.ShapeDtypeStruct((T, D), BF)
    return pl.pallas_call(
        finish_kernel,
        out_shape=(jax.ShapeDtypeStruct((T, H * D), BF), grad, grad),
        in_specs=[VM] * 4,
        out_specs=(VM,) * 3,
        compiler_params=pltpu.CompilerParams(vmem_limit_bytes=VMEM_LIMIT),
        name="finish",
    )(*arrays)


def local(queries, keys, values, outputs, out_grad, lse, block_order, doc_lengths):
    swap = [(i, i ^ 4) for i in range(2 * PLANE)]
    pair_lse = lax.ppermute(lse, "ctx", swap)
    pair_q = lax.ppermute(queries, "ctx", swap)
    pair_g = lax.ppermute(out_grad, "ctx", swap)
    ka, va, qa, ga, qt, gt, lc, dc, delta = gather(keys, values, queries, out_grad, outputs, lse)
    pair_delta = lax.ppermute(delta, "ctx", swap)
    k = ka.reshape(2 * PLANE, B, D)
    v = va.reshape(2 * PLANE, B, D)
    dq_own, dk, dv = attend(True, block_order, doc_lengths, qa, ga, qt, gt, lc, dc, k, v)
    dq_pair, dk, dv = attend(False, block_order, doc_lengths, pair_q, pair_g, pair_lse, pair_delta, k, v, dk, dv)
    back, k_sum, v_sum = reduce(dq_pair, dk, dv)
    return finish(dq_own, back, k_sum, v_sum)


def solution(mesh):
    rows = P(("dp", "ctx"), None)
    return jax.shard_map(
        local,
        mesh=mesh,
        in_specs=(rows, rows, rows, rows, rows, P(None, ("dp", "ctx")), P("dp"), P("dp")),
        out_specs=(rows, rows, rows),
        check_vma=False,
    )
```

time: 75 us -> 71.2 us (0.949)
  Pallas kernels: 74.2 us -> 60.1 us
  starting transfers between devices: 0 us -> 9.27 us
  local copies, waits for them, and re-layouts: 0 us -> 0.95 us
    pallas_call x1, Pallas kernels: 32.2 us -> 20.5 us  [gather(): pl.pallas_call(gather_kernel, out_shape=(pltpu.VMEM((PLANE, T, D), BF), p...]
    ppermute x0 -> x4, starting transfers between devices: none -> 9.27 us  [the longest x1 3.36 us: local(): pair_q = lax.ppermute(queries, 'ctx', swap)]
    pallas_call x2 -> x3, Pallas kernels: 41 us -> 38.6 us  [the longest x1 26.3 us: reduce(): pl.pallas_call(reduce_kernel, out_shape=(pltpu.VMEM((2, H * B, D), BF), p...]
    unnamed x0 -> x4, local copies, waits for them, and re-layouts: none -> 0.95 us
  transfers between devices with their start and end apart: 0 -> 4, of which waited for: 0 -> 0; matrix products, arithmetic and copies ran while one was open for 0% -> 0% of each run, Pallas kernels for 0% -> 35%
where the time goes in v3:
time: 71.2 us; the launch traced here: 71 us
  Pallas kernels  60.1 us (84%)
  starting transfers between devices  9.27 us (13%)
  local copies, waits for them, and re-layouts  0.95 us (1%)
    pallas_call x1, Pallas kernels, reduce(): pl.pallas_call(reduce_kernel, out_shape=(pltpu.VMEM((2, H * B, D), BF), p...  26.3 us
    pallas_call x1, Pallas kernels, gather(): pl.pallas_call(gather_kernel, out_shape=(pltpu.VMEM((PLANE, T, D), BF), p...  20.5 us
    pallas_call x2, Pallas kernels, attend(): pl.pallas_call(functools.partial(attend_kernel, own), out_shape=(pltpu.VM...  12.3 us
    ppermute x1, starting transfers between devices, local(): pair_q = lax.ppermute(queries, 'ctx', swap)  3.36 us
    ppermute x1, starting transfers between devices, local(): pair_lse = lax.ppermute(lse, 'ctx', swap)  3.28 us
    ppermute x1, starting transfers between devices, local(): pair_delta = lax.ppermute(delta, 'ctx', swap)  2.39 us
  transfers between devices with their start and end apart: 4, of which 0 were waited for; matrix products, arithmetic and copies ran while one was open for 0% of the time, Pallas kernels for 35%

profile of v3, /device:TPU:0, one launch (start us, length us, event | category | flops | bytes accessed | tf_op | source)
XLA Modules:
  0.0 71.0 jit_solution(2874938898761400777)
XLA Ops:
  0.6 3.4 %collective-permute-start = (bf16[256,1024]{1,0:T(8,128)(2,1)}, bf16[256,1024]{1,0:T(8,128)(2,1)S(1)}, u32[]{:S(2)}, u32[]{:S(2)}) collective-permute-start(bf16[256,1024]{1,0:T(8,128)(2,1)} %q_ref.1), channel_id=1, source_target_pairs={{0,16},{4,20},{8,24},{12,28},{16,0},{20,4},{24,8},{28,12},{32,48},... | collective-permute-start | bytes 1572872 | tf_op jit(solution)/shard_map/ppermute | solution.py:469
  4.0 0.3 collective-permute-start.1
  4.2 3.3 %collective-permute-start.2 = (f32[8,256]{1,0:T(8,128)}, f32[8,256]{1,0:T(8,128)S(1)}, u32[]{:S(2)}, u32[]{:S(2)}) collective-permute-start(f32[8,256]{1,0:T(8,128)} %lse_ref.1), channel_id=1, source_target_pairs={{0,16},{4,20},{8,24},{12,28},{16,0},{20,4},{24,8},{28,12},{32,48},... | collective-permute-start | bytes 24584 | tf_op jit(solution)/shard_map/ppermute | solution.py:468
  7.5 20.5 %gather_rows.1 = (bf16[16,256,128]{2,1,0:T(8,128)(2,1)S(1)}, bf16[16,256,128]{2,1,0:T(8,128)(2,1)S(1)}, bf16[2,128,1024]{2,1,0:T(8,128)(2,1)S(1)}, bf16[2,128,10...) custom-call(bf16[256,128]{1,0:T(8,128)(2,1)} %k_ref.1, ...), custom_call_target="tpu_custom_call" | custom-call | tf_op jit(solution)/shard_map/gather_rows/pallas_call | solution.py:179
  28.0 2.4 %collective-permute-start.3 = (f32[8,256]{1,0:T(8,128)S(1)}, f32[8,256]{1,0:T(8,128)S(1)}, u32[]{:S(2)}, u32[]{:S(2)}) collective-permute-start(f32[8,256]{1,0:T(8,128)S(1)} %get-tuple-element.30), channel_id=1, source_target_pairs={{0,16},{4,20},{8,24},{12,28},{16,0},{20,4},{24,8},{28,12},{32,48},... | collective-permute-start | bytes 24584 | tf_op jit(solution)/shard_map/ppermute | solution.py:472
  30.4 4.3 %attend_own.1 = (f32[2,1024,128]{2,1,0:T(8,128)S(1)}, f32[32,128,128]{2,1,0:T(8,128)S(1)}, f32[32,128,128]{2,1,0:T(8,128)S(1)}) custom-call(s32[64]{0:T(128)} %order.3, s32[16]{0:T(128)} %lens.3, bf16[2,128,1024]{2,1,0:T(8,128)(2,1)S(1)} %get-tuple-element.21.refs_0_, bf16[2,128,1024]{2,1,0:T(8,128)(2,1)S(1)} %get-tuple-element.22.refs_1_, ...), custom_call_target="tpu_custom_call" | custom-call | tf_op jit(solution)/shard_map/attend_own/pallas_call | solution.py:348
  34.7 0.0 collective-permute-done.2.refs_2_
  34.7 0.0 collective-permute-done.3.refs_3_
  34.7 0.0 collective-permute-done.refs_0_
  34.7 0.0 copy-start
  34.7 0.0 collective-permute-done.1.refs_1_
  34.7 0.0 copy-start.1
  34.7 0.8 %copy-done = bf16[256,1024]{1,0:T(8,128)(2,1)} copy-done((bf16[256,1024]{1,0:T(8,128)(2,1)}, bf16[256,1024]{1,0:T(8,128)(2,1)S(1)}, u32[]{:S(2)}) %copy-start) | copy-done | bytes 524312
  35.5 0.2 copy-done.1
  35.7 8.0 %attend_pair.1 = (bf16[2,1024,128]{2,1,0:T(8,128)(2,1)S(1)}, f32[32,128,128]{2,1,0:T(8,128)S(1)}, f32[32,128,128]{2,1,0:T(8,128)S(1)}) custom-call(s32[64]{0:T(128)} %order.3, s32[16]{0:T(128)} %lens.3, bf16[256,1024]{1,0:T(8,128)(2,1)} %copy-done, bf16[256,1024]{1,0:T(8,128)(2,1)} %copy-done.1, ...), custom_call_target="tpu_custom_call", output_to_operand_aliasing={{1}: (8, {}), {2}: (9, {})} | custom-call | tf_op jit(solution)/shard_map/attend_pair/pallas_call | solution.py:348
  43.7 26.3 %reduce_rows.1 = (bf16[2,1024,128]{2,1,0:T(8,128)(2,1)S(1)}, f32[2,128,128]{2,1,0:T(8,128)S(1)}, f32[2,128,128]{2,1,0:T(8,128)S(1)}) custom-call(bf16[2,1024,128]{2,1,0:T(8,128)(2,1)S(1)} %get-tuple-element.33.dq_ref, f32[16,2,128,128]{3,2,1,0:T(8,128)S(1)} %bitcast.4, f32[16,2,128,128]{3,2,1,0:T(8,128)S(1)} %bitcast.5), custom_call_target="tpu_custom_call" | custom-call | tf_op jit(solution)/shard_map/reduce_rows/pallas_call | solution.py:420
  70.0 1.0 %finish.1 = (bf16[256,1024]{1,0:T(8,128)(2,1)}, bf16[256,128]{1,0:T(8,128)(2,1)}, bf16[256,128]{1,0:T(8,128)(2,1)}) custom-call(f32[2,1024,128]{2,1,0:T(8,128)S(1)} %get-tuple-element.29.dq_own, bf16[2,1024,128]{2,1,0:T(8,128)(2,1)S(1)} %get-tuple-element.36.back, f32[2,128,128]{2,1,0:T(8,128)S(1)} %get-tuple-element.37.k_sum, ...), custom_call_target="tpu_custom_call" | custom-call | tf_op jit(solution)/shard_map/finish/pallas_call | solution.py:456
Async XLA Ops:
  0.6 34.1 %collective-permute-start = (bf16[256,1024]{1,0:T(8,128)(2,1)}, bf16[256,1024]{1,0:T(8,128)(2,1)S(1)}, u32[]{:S(2)}, u32[]{:S(2)}) collective-permute-start(bf16[256,1024]{1,0:T(8,128)(2,1)} %q_ref.1), channel_id=1, source_target_pairs={{0,16},{4,20},{8,24},{12,28},{16,0},{20,4},{24,8},{28,12},{32,48},... | collective-permute-start | bytes 1572872 | tf_op jit(solution)/shard_map/ppermute | solution.py:469
  4.0 30.7 %collective-permute-start.1 = (bf16[256,1024]{1,0:T(8,128)(2,1)}, bf16[256,1024]{1,0:T(8,128)(2,1)S(1)}, u32[]{:S(2)}, u32[]{:S(2)}) collective-permute-start(bf16[256,1024]{1,0:T(8,128)(2,1)} %g_ref.1), channel_id=1, source_target_pairs={{0,16},{4,20},{8,24},{12,28},{16,0},{20,4},{24,8},{28,12},{32,48},... | collective-permute-start | bytes 1572872 | tf_op jit(solution)/shard_map/ppermute | solution.py:470
  4.2 30.4 %collective-permute-start.2 = (f32[8,256]{1,0:T(8,128)}, f32[8,256]{1,0:T(8,128)S(1)}, u32[]{:S(2)}, u32[]{:S(2)}) collective-permute-start(f32[8,256]{1,0:T(8,128)} %lse_ref.1), channel_id=1, source_target_pairs={{0,16},{4,20},{8,24},{12,28},{16,0},{20,4},{24,8},{28,12},{32,48},... | collective-permute-start | bytes 24584 | tf_op jit(solution)/shard_map/ppermute | solution.py:468
  28.0 6.7 %collective-permute-start.3 = (f32[8,256]{1,0:T(8,128)S(1)}, f32[8,256]{1,0:T(8,128)S(1)}, u32[]{:S(2)}, u32[]{:S(2)}) collective-permute-start(f32[8,256]{1,0:T(8,128)S(1)} %get-tuple-element.30), channel_id=1, source_target_pairs={{0,16},{4,20},{8,24},{12,28},{16,0},{20,4},{24,8},{28,12},{32,48},... | collective-permute-start | bytes 24584 | tf_op jit(solution)/shard_map/ppermute | solution.py:472
  34.7 0.8 %copy-start = (bf16[256,1024]{1,0:T(8,128)(2,1)}, bf16[256,1024]{1,0:T(8,128)(2,1)S(1)}, u32[]{:S(2)}) copy-start(bf16[256,1024]{1,0:T(8,128)(2,1)S(1)} %collective-permute-done.refs_0_) | copy-start | bytes 1572868
  34.7 1.0 %copy-start.1 = (bf16[256,1024]{1,0:T(8,128)(2,1)}, bf16[256,1024]{1,0:T(8,128)(2,1)S(1)}, u32[]{:S(2)}) copy-start(bf16[256,1024]{1,0:T(8,128)(2,1)S(1)} %collective-permute-done.1.refs_1_) | copy-start | bytes 1572868

commit v4 on v3

--- a/solution.py
+++ b/solution.py
@@ -58,38 +58,84 @@
     pl.semaphore_wait(pltpu.get_barrier_semaphore(), 7)
 
 
-def widen(ref, dst):
-    head_of = lax.broadcasted_iota(I32, (3 * H, D), 0) % H
+def pieces(whole):
+    hi = whole.astype(BF)
+    left = whole - hi.astype(F32)
+    mid = left.astype(BF)
+    return hi, mid, (left - mid.astype(F32)).astype(BF)
+
+
+def pack_kernel(q_ref, g_ref, o_ref, lse_ref, packed, outs, lses, sems):
+    copies = [
+        pltpu.make_async_copy(g_ref, packed.at[pl.ds(T, T)], sems.at[0]),
+        pltpu.make_async_copy(o_ref, outs, sems.at[1]),
+        pltpu.make_async_copy(lse_ref, lses, sems.at[2]),
+        pltpu.make_async_copy(q_ref, packed.at[pl.ds(0, T)], sems.at[3]),
+    ]
+    for copy in copies:
+        copy.start()
+    for copy in copies[:3]:
+        copy.wait()
+    ones = jnp.ones((8, D), BF)
+    deltas = []
+    for h in range(H):
+        cols = slice(h * D, (h + 1) * D)
+        prod = packed[T : 2 * T, cols].astype(F32) * outs[:, cols].astype(F32)
+        hi = prod.astype(BF)
+        lo = (prod - hi.astype(F32)).astype(BF)
+        deltas.append((dot(ones, hi, 1, 1) + dot(ones, lo, 1, 1))[0:1, :])
+    whole = jnp.concatenate([jnp.minimum(lses[...], 1e30)] + deltas, axis=0)
+    for i, piece in enumerate(pieces(whole)):
+        packed[2 * T :, i * T : (i + 1) * T] = piece
+    packed[2 * T :, 3 * T :] = jnp.zeros((2 * H, T), BF)
+    copies[3].wait()
+
+
+def pack(queries, out_grad, outputs, lse):
+    return pl.pallas_call(
+        pack_kernel,
+        out_shape=pltpu.VMEM((2 * T + 2 * H, H * D), BF),
+        in_specs=[ANY] * 4,
+        out_specs=VM,
+        scratch_shapes=[
+            pltpu.VMEM((T, H * D), BF),
+            pltpu.VMEM((H, T), F32),
+            pltpu.SemaphoreType.DMA((4,)),
+        ],
+        compiler_params=pltpu.CompilerParams(vmem_limit_bytes=VMEM_LIMIT),
+        name="pack_rows",
+    )(*[stay(t) for t in (queries, out_grad, outputs, lse)])
+
+
+def widen(packed, lc, dc):
+    which = lax.broadcasted_iota(I32, (6 * H, D), 0) % (2 * H)
     for blk in (0, 1):
-        whole = jnp.minimum(ref[:, blk * B : (blk + 1) * B], 1e30)
-        hi = whole.astype(BF)
-        left = whole - hi.astype(F32)
-        mid = left.astype(BF)
-        lo = (left - mid.astype(F32)).astype(BF)
-        parts = jnp.concatenate([hi.astype(F32), mid.astype(F32), lo.astype(F32)], axis=0).astype(BF)
-        for h in range(H):
-            select = jnp.where(head_of == h, 1.0, 0.0).astype(BF)
-            dst[blk, h * D : (h + 1) * D, :] = dot(parts, select, 0, 0)
+        parts = [packed[2 * T :, i * T + blk * B : i * T + (blk + 1) * B] for i in range(3)]
+        parts = jnp.concatenate(parts, axis=0)
+        for h in range(2 * H):
+            select = jnp.where(which == h, 1.0, 0.0).astype(BF)
+            (lc, dc)[h // H][blk, h % H * D : (h % H + 1) * D, :] = dot(parts, select, 0, 0)
+
+
+def turn(packed, qt, gt):
+    for dst, first in ((qt, 0), (gt, T)):
+        for blk in (0, 1):
+            for h in range(H):
+                cols = slice(h * D, (h + 1) * D)
+                dst[blk, :, cols] = packed[first + blk * B : first + (blk + 1) * B, cols].T
 
 
 def gather_kernel(
-    k_ref, v_ref, q_ref, g_ref, o_ref, lse_ref, ka, va, qa, ga, qt, gt, lc, dc, delta,
-    outs, lses, own_sem, s1, r1, s2, r2, s3, r3,
+    k_ref, v_ref, packed, ka, va, qt, gt, lc, dc, own_sem, s1, r1, s2, r2, s3, r3,
 ):
     z, y, x = coords()
     here = z * RING + x
-
-    def keep(src, dst, sem):
-        copy = pltpu.make_async_copy(src, dst, sem)
+    greet_signal(z, y, x)
+    own = []
+    for a, (src, dst) in enumerate(((k_ref, ka), (v_ref, va))):
+        copy = pltpu.make_async_copy(src, dst.at[here], own_sem.at[a])
         copy.start()
-        return copy
-
-    grads_in = [keep(g_ref.at[pl.ds(blk * B, B)], ga.at[blk], own_sem.at[blk]) for blk in (0, 1)]
-    outs_in = keep(o_ref, outs, own_sem.at[2])
-    lse_in = keep(lse_ref, lses, own_sem.at[3])
-    rows_in = [keep(q_ref.at[pl.ds(blk * B, B)], qa.at[blk], own_sem.at[4 + blk]) for blk in (0, 1)]
-    own = [keep(src, dst.at[here], own_sem.at[6 + a]) for a, (src, dst) in enumerate(((k_ref, ka), (v_ref, va)))]
-    greet_signal(z, y, x)
+        own.append(copy)
     greet_wait()
 
     def send(src, dst, ssem, rsem, to):
@@ -131,18 +177,6 @@
             first[a, s].wait_recv()
             spread(a, s)
 
-    for copy in grads_in + [outs_in]:
-        copy.wait()
-    ones = jnp.ones((8, D), BF)
-    for h in range(H):
-        cols = slice(h * D, (h + 1) * D)
-        grad = jnp.concatenate([ga[0, :, cols], ga[1, :, cols]], axis=0)
-        prod = grad.astype(F32) * outs[:, cols].astype(F32)
-        hi = prod.astype(BF)
-        lo = (prod - hi.astype(F32)).astype(BF)
-        total = dot(ones, hi, 1, 1) + dot(ones, lo, 1, 1)
-        delta[h : h + 1, :] = total[0:1, :]
-
     def relay(s):
         for e, half in ((1, 0), (3, 1)):
             for a in (0, 1):
@@ -150,23 +184,13 @@
                 part = alls[a].at[slot_from(a, s, e), pl.ds(half * B, B)]
                 third[a, s, half] = send(part, part, s3.at[a, s, half], r3.at[a, s, half], second_peer(a, e))
 
-    def turn(src, dst, blk):
-        for h in range(H):
-            cols = slice(h * D, (h + 1) * D)
-            dst[blk, :, cols] = src[blk, :, cols].T
-
     relay(0)
-    for copy in rows_in + own:
+    for copy in own:
         copy.wait()
-    turn(qa, qt, 0)
-    turn(ga, gt, 0)
     relay(1)
-    turn(qa, qt, 1)
-    turn(ga, gt, 1)
+    widen(packed, lc, dc)
     relay(3)
-    lse_in.wait()
-    widen(lses, lc)
-    widen(delta, dc)
+    turn(packed, qt, gt)
     relay(2)
     for copy in third.values():
         copy.wait_recv()
@@ -174,34 +198,28 @@
         copy.wait_send()
 
 
-def gather(keys, values, queries, out_grad, outputs, lse):
+def gather(keys, values, packed):
     dma = pltpu.SemaphoreType.DMA
     return pl.pallas_call(
         gather_kernel,
         out_shape=(
             pltpu.VMEM((PLANE, T, D), BF),
             pltpu.VMEM((PLANE, T, D), BF),
-            pltpu.VMEM((2, B, H * D), BF),
-            pltpu.VMEM((2, B, H * D), BF),
             pltpu.VMEM((2, D, H * B), BF),
             pltpu.VMEM((2, D, H * B), BF),
             pltpu.VMEM((2, H * B, D), F32),
             pltpu.VMEM((2, H * B, D), F32),
-            pltpu.VMEM((H, T), F32),
         ),
-        in_specs=[ANY] * 6,
-        out_specs=(VM,) * 9,
+        in_specs=[ANY] * 2 + [VM],
+        out_specs=(VM,) * 6,
         scratch_shapes=[
-            pltpu.VMEM((T, H * D), BF),
-            pltpu.VMEM((H, T), F32),
-            dma((8,)), dma((2, 3)), dma((2, 3)), dma((2, 4, 3)), dma((2, 4, 3)),
-            dma((2, 4, 2)), dma((2, 4, 2)),
+            dma((2,)), dma((2, 3)), dma((2, 3)), dma((2, 4, 3)), dma((2, 4, 3)), dma((2, 4, 2)), dma((2, 4, 2)),
         ],
         compiler_params=pltpu.CompilerParams(
             collective_id=0, has_side_effects=True, vmem_limit_bytes=VMEM_LIMIT
         ),
         name="gather_rows",
-    )(*[stay(t) for t in (keys, values, queries, out_grad, outputs, lse)])
+    )(stay(keys), stay(values), packed)
 
 
 KEYS = 36
@@ -210,17 +228,11 @@
 
 def attend_kernel(own, order, lens, *refs):
     if own:
-        qa, ga, qt, gt, lc, dc, k_ref, v_ref, dqa, dk, dv = refs[:11]
-        slots, places, qfrom, qbase, pbuf, dbuf = refs[11:]
+        packed, k_ref, v_ref, qt, gt, lc, dc, dqa, dk, dv = refs[:10]
+        slots, places, qfrom, qbase, pbuf, dbuf = refs[10:]
     else:
-        q_hbm, g_hbm, lse_ref, delta_ref, k_ref, v_ref, _, _, dq_out, dk, dv = refs[:11]
-        slots, places, qfrom, qbase, pbuf, dbuf, qa, ga, qt, gt, lc, dc, dqa, sems = refs[11:]
-        loads = []
-        for blk in (0, 1):
-            for i, (src, dst) in enumerate(((q_hbm, qa), (g_hbm, ga))):
-                copy = pltpu.make_async_copy(src.at[pl.ds(blk * B, B)], dst.at[blk], sems.at[2 * blk + i])
-                copy.start()
-                loads.append(copy)
+        packed, k_ref, v_ref, _, _, dq_out, dk, dv = refs[:8]
+        slots, places, qfrom, qbase, pbuf, dbuf, qt, gt, lc, dc, dqa = refs[8:]
     me = lax.axis_index("ctx")
     plane = (me // 4) % 2
     owner = me if own else me + 4 - 8 * plane
@@ -265,14 +277,8 @@
         dk[...] = jnp.zeros_like(dk)
         dv[...] = jnp.zeros_like(dv)
     else:
-        widen(lse_ref, lc)
-        widen(delta_ref, dc)
-        for blk in (0, 1):
-            for src, dst, copy in ((qa, qt, loads[2 * blk]), (ga, gt, loads[2 * blk + 1])):
-                copy.wait()
-                for h in range(H):
-                    cols = slice(h * D, (h + 1) * D)
-                    dst[blk, :, cols] = src[blk, :, cols].T
+        widen(packed, lc, dc)
+        turn(packed, qt, gt)
     scale = jnp.float32(D**-0.5)
     across = lax.broadcasted_iota(I32, (1, B), 1)
 
@@ -296,8 +302,10 @@
         for two in range(4):
             cols = slice(two * 256, (two + 1) * 256)
             heads = [slice((2 * two + i) * D, (2 * two + i + 1) * D) for i in (0, 1)]
-            score = dot(jnp.concatenate([qa[blk, :, c] for c in heads], axis=0), kk, 1, 1)
-            dprob = dot(jnp.concatenate([ga[blk, :, c] for c in heads], axis=0), vv, 1, 1)
+            q_rows = pl.ds(pl.multiple_of(blk * B, B), B)
+            g_rows = pl.ds(pl.multiple_of(T + blk * B, B), B)
+            score = dot(jnp.concatenate([packed[q_rows, c] for c in heads], axis=0), kk, 1, 1)
+            dprob = dot(jnp.concatenate([packed[g_rows, c] for c in heads], axis=0), vv, 1, 1)
             less = lc[blk, cols, :]
             delta = dc[blk, cols, :]
             prob = jnp.where(allowed, jnp.exp(score * scale - jnp.concatenate([less, less], axis=1)), 0.0)
@@ -329,7 +337,7 @@
 
 def attend(own, order, lens, *arrays):
     sums = pltpu.VMEM((2 * PLANE, D, B), F32)
-    rows = pltpu.VMEM((2, B, H * D), BF)
+    rows = pltpu.VMEM((2, H * B, D), F32)
     cols = pltpu.VMEM((2, D, H * B), BF)
     scratch = [
         pltpu.SMEM((2 * KEYS,), I32),
@@ -339,19 +347,15 @@
         pltpu.VMEM((2, H * B, 2 * B), BF),
         pltpu.VMEM((2, H * B, 2 * B), BF),
     ]
-    if own:
-        specs = [SM] * 2 + [VM] * 8
-    else:
-        specs = [SM] * 2 + [ANY] * 2 + [VM] * 6
-        scratch += [rows, rows, cols, cols] + [pltpu.VMEM((2, H * B, D), F32)] * 3 + [pltpu.SemaphoreType.DMA((4,))]
-        arrays = [stay(t) for t in arrays[:2]] + list(arrays[2:])
+    if not own:
+        scratch += [cols, cols, rows, rows, rows]
     return pl.pallas_call(
         functools.partial(attend_kernel, own),
         out_shape=(pltpu.VMEM((2, H * B, D), F32 if own else BF), sums, sums),
-        in_specs=specs,
+        in_specs=[SM] * 2 + [VM] * len(arrays),
         out_specs=(VM,) * 3,
         scratch_shapes=scratch,
-        input_output_aliases={} if own else {8: 1, 9: 2},
+        input_output_aliases={} if own else {5: 1, 6: 2},
         compiler_params=pltpu.CompilerParams(vmem_limit_bytes=VMEM_LIMIT),
         name="attend_own" if own else "attend_pair",
     )(stay(order), stay(lens), *arrays)
@@ -465,15 +469,13 @@
 
 def local(queries, keys, values, outputs, out_grad, lse, block_order, doc_lengths):
     swap = [(i, i ^ 4) for i in range(2 * PLANE)]
-    pair_lse = lax.ppermute(lse, "ctx", swap)
-    pair_q = lax.ppermute(queries, "ctx", swap)
-    pair_g = lax.ppermute(out_grad, "ctx", swap)
-    ka, va, qa, ga, qt, gt, lc, dc, delta = gather(keys, values, queries, out_grad, outputs, lse)
-    pair_delta = lax.ppermute(delta, "ctx", swap)
+    packed = pack(queries, out_grad, outputs, lse)
+    other = lax.ppermute(packed, "ctx", swap)
+    ka, va, qt, gt, lc, dc = gather(keys, values, packed)
     k = ka.reshape(2 * PLANE, B, D)
     v = va.reshape(2 * PLANE, B, D)
-    dq_own, dk, dv = attend(True, block_order, doc_lengths, qa, ga, qt, gt, lc, dc, k, v)
-    dq_pair, dk, dv = attend(False, block_order, doc_lengths, pair_q, pair_g, pair_lse, pair_delta, k, v, dk, dv)
+    dq_own, dk, dv = attend(True, block_order, doc_lengths, packed, k, v, qt, gt, lc, dc)
+    dq_pair, dk, dv = attend(False, block_order, doc_lengths, other, k, v, dk, dv)
     back, k_sum, v_sum = reduce(dq_pair, dk, dv)
     return finish(dq_own, back, k_sum, v_sum)
 

time: 71.2 us -> 66.3 us (0.931)
  starting transfers between devices: 9.27 us -> 3.36 us
  Pallas kernels: 60.1 us -> 61.4 us
  local copies, waits for them, and re-layouts: 0.95 us -> 0 us
    ppermute x4 -> x1, starting transfers between devices: 9.27 us -> 3.36 us  [local(): other = lax.ppermute(packed, 'ctx', swap)]
    pallas_call x1, Pallas kernels: 26.3 us -> 22 us  [reduce(): pl.pallas_call(reduce_kernel, out_shape=(pltpu.VMEM((2, H * B, D), BF), p...]
    pallas_call x2, Pallas kernels: 12.3 us -> 16 us  [attend(): pl.pallas_call(functools.partial(attend_kernel, own), out_shape=(pltpu.VM...]
    pallas_call x0 -> x1, Pallas kernels: none -> 1.66 us  [pack(): pl.pallas_call(pack_kernel, out_shape=pltpu.VMEM((2 * T + 2 * H, H * D),...]
    unnamed x4 -> x0, local copies, waits for them, and re-layouts: 0.95 us -> none
  transfers between devices with their start and end apart: 4 -> 1, of which waited for: 0 -> 0; matrix products, arithmetic and copies ran while one was open for 0% -> 0% of each run, Pallas kernels for 35% -> 43%
where the time goes in v4:
time: 66.3 us; the launch traced here: 65.4 us
  Pallas kernels  61.4 us (93%)
  starting transfers between devices  3.36 us (5%)
  between operations  0.68 us (1%)
    pallas_call x1, Pallas kernels, reduce(): pl.pallas_call(reduce_kernel, out_shape=(pltpu.VMEM((2, H * B, D), BF), p...  22 us
    pallas_call x1, Pallas kernels, gather(): pl.pallas_call(gather_kernel, out_shape=(pltpu.VMEM((PLANE, T, D), BF), p...  20.7 us
    pallas_call x2, Pallas kernels, attend(): pl.pallas_call(functools.partial(attend_kernel, own), out_shape=(pltpu.VM...  16 us
    ppermute x1, starting transfers between devices, local(): other = lax.ppermute(packed, 'ctx', swap)  3.36 us
    pallas_call x1, Pallas kernels, pack(): pl.pallas_call(pack_kernel, out_shape=pltpu.VMEM((2 * T + 2 * H, H * D),...  1.66 us
  transfers between devices with their start and end apart: 1, of which 0 were waited for; matrix products, arithmetic and copies ran while one was open for 0% of the time, Pallas kernels for 43%

profile of v4, /device:TPU:0, one launch (start us, length us, event | category | flops | bytes accessed | tf_op | source)
XLA Modules:
  0.0 65.4 jit_solution(392143990663408792)
XLA Ops:
  0.6 1.7 %pack_rows.1.packed.refs_0_ = bf16[528,1024]{1,0:T(8,128)(2,1)S(1)} custom-call(bf16[256,1024]{1,0:T(8,128)(2,1)} %q_ref.1, bf16[256,1024]{1,0:T(8,128)(2,1)} %g_ref.1, bf16[256,1024]{1,0:T(8,128)(2,1)} %o_ref.1, f32[8,256]{1,0:T(8,128)} %lse_ref.1), custom_call_target="tpu_custom_call" | custom-call | tf_op jit(solution)/shard_map/pack_rows/pallas_call | solution.py:95
  2.3 3.4 %collective-permute-start = (bf16[528,1024]{1,0:T(8,128)(2,1)S(1)}, bf16[528,1024]{1,0:T(8,128)(2,1)S(1)}, u32[]{:S(2)}, u32[]{:S(2)}) collective-permute-start(bf16[528,1024]{1,0:T(8,128)(2,1)S(1)} %pack_rows.1.packed.refs_0_), channel_id=1, source_target_pairs={{0,16},{4,20},{8,24},{12,28},{16,0},{20,4},{24,8},{28,12},{32,48},... | collective-permute-start | bytes 3244040 | tf_op jit(solution)/shard_map/ppermute | solution.py:473
  5.7 20.7 %gather_rows.1 = (bf16[16,256,128]{2,1,0:T(8,128)(2,1)S(1)}, bf16[16,256,128]{2,1,0:T(8,128)(2,1)S(1)}, bf16[2,128,1024]{2,1,0:T(8,128)(2,1)S(1)}, bf16[2,128,10...) custom-call(bf16[256,128]{1,0:T(8,128)(2,1)} %k_ref.1, bf16[256,128]{1,0:T(8,128)(2,1)} %v_ref.1, ...), custom_call_target="tpu_custom_call" | custom-call | tf_op jit(solution)/shard_map/gather_rows/pallas_call | solution.py:203
  26.3 7.1 %attend_own.1 = (f32[2,1024,128]{2,1,0:T(8,128)S(1)}, f32[32,128,128]{2,1,0:T(8,128)S(1)}, f32[32,128,128]{2,1,0:T(8,128)S(1)}) custom-call(s32[64]{0:T(128)} %order.3, s32[16]{0:T(128)} %lens.3, bf16[528,1024]{1,0:T(8,128)(2,1)S(1)} %pack_rows.1.packed.refs_0_, bf16[32,128,128]{2,1,0:T(8,128)(2,1)S(1)} %bitcast.6, bf16[32,128,128]{2,1,0:T(8,128)(2,1)S(1)} %bitcast.8, ...), custom_call_target="tpu_custom_call" | custom-call | tf_op jit(solution)/shard_map/attend_own/pallas_call | solution.py:352
  33.5 0.0 collective-permute-done.refs_0_
  33.5 8.8 %attend_pair.1 = (bf16[2,1024,128]{2,1,0:T(8,128)(2,1)S(1)}, f32[32,128,128]{2,1,0:T(8,128)S(1)}, f32[32,128,128]{2,1,0:T(8,128)S(1)}) custom-call(s32[64]{0:T(128)} %order.3, s32[16]{0:T(128)} %lens.3, bf16[528,1024]{1,0:T(8,128)(2,1)S(1)} %collective-permute-done.refs_0_, ...), custom_call_target="tpu_custom_call", output_to_operand_aliasing={{1}: (5, {}), {2}: (6, {})} | custom-call | tf_op jit(solution)/shard_map/attend_pair/pallas_call | solution.py:352
  42.3 22.0 %reduce_rows.1 = (bf16[2,1024,128]{2,1,0:T(8,128)(2,1)S(1)}, f32[2,128,128]{2,1,0:T(8,128)S(1)}, f32[2,128,128]{2,1,0:T(8,128)S(1)}) custom-call(bf16[2,1024,128]{2,1,0:T(8,128)(2,1)S(1)} %get-tuple-element.27.dq_ref, f32[16,2,128,128]{3,2,1,0:T(8,128)S(1)} %bitcast.4, f32[16,2,128,128]{3,2,1,0:T(8,128)S(1)} %bitcast.5), custom_call_target="tpu_custom_call" | custom-call | tf_op jit(solution)/shard_map/reduce_rows/pallas_call | solution.py:424
  64.4 1.0 %finish.1 = (bf16[256,1024]{1,0:T(8,128)(2,1)}, bf16[256,128]{1,0:T(8,128)(2,1)}, bf16[256,128]{1,0:T(8,128)(2,1)}) custom-call(f32[2,1024,128]{2,1,0:T(8,128)S(1)} %get-tuple-element.24.dq_own, bf16[2,1024,128]{2,1,0:T(8,128)(2,1)S(1)} %get-tuple-element.30.back, f32[2,128,128]{2,1,0:T(8,128)S(1)} %get-tuple-element.31.k_sum, ...), custom_call_target="tpu_custom_call" | custom-call | tf_op jit(solution)/shard_map/finish/pallas_call | solution.py:460
Async XLA Ops:
  2.3 31.2 %collective-permute-start = (bf16[528,1024]{1,0:T(8,128)(2,1)S(1)}, bf16[528,1024]{1,0:T(8,128)(2,1)S(1)}, u32[]{:S(2)}, u32[]{:S(2)}) collective-permute-start(bf16[528,1024]{1,0:T(8,128)(2,1)S(1)} %pack_rows.1.packed.refs_0_), channel_id=1, source_target_pairs={{0,16},{4,20},{8,24},{12,28},{16,0},{20,4},{24,8},{28,12},{32,48},... | collective-permute-start | bytes 3244040 | tf_op jit(solution)/shard_map/ppermute | solution.py:473

commit v5 on v4

v5 whole, which is shorter than its diff:
```python
import functools
import math

import jax
import jax.numpy as jnp
from jax import lax
from jax.experimental import pallas as pl
from jax.experimental.pallas import tpu as pltpu
from jax.sharding import PartitionSpec as P

BF = jnp.bfloat16
F32 = jnp.float32
I32 = jnp.int32
MESH = pl.DeviceIdType.MESH
VM = pl.BlockSpec(memory_space=pltpu.VMEM)
SM = pl.BlockSpec(memory_space=pltpu.SMEM)
ANY = pl.BlockSpec(memory_space=pl.ANY)

RING = 4
PLANE = RING * RING
T = 256
B = 128
H = 8
D = 128
VMEM_LIMIT = 32 * 2**20
LOG2E = math.log2(math.e)


def dot(a, b, ca, cb):
    return lax.dot_general(a, b, (((ca,), (cb,)), ((), ())), preferred_element_type=F32)


def stay(array):
    return pltpu.with_memory_space_constraint(array, pltpu.HBM)


def coords():
    me = lax.axis_index("ctx")
    return me // 8, (me // 4) % 2, me % 4


def ident(z, y, x):
    return {"ctx": z * 8 + y * 4 + x}


def step_of(v, d):
    return lax.rem(v + d, RING)


def greet_signal(z, y, x):
    barrier = pltpu.get_barrier_semaphore()
    others = [ident(z, y, step_of(x, d)) for d in (1, 2, 3)]
    others += [ident(step_of(z, d), y, x) for d in (1, 2, 3)]
    others.append(ident(z, 1 - y, x))
    for other in others:
        pl.semaphore_signal(barrier, inc=1, device_id=other, device_id_type=MESH)


def greet_wait():
    pl.semaphore_wait(pltpu.get_barrier_semaphore(), 7)


def pieces(whole):
    hi = whole.astype(BF)
    left = whole - hi.astype(F32)
    mid = left.astype(BF)
    return hi, mid, (left - mid.astype(F32)).astype(BF)


def widen(stats, side, blk, lc, dc, to):
    which = lax.broadcasted_iota(I32, (6 * H, D), 0) % (2 * H)
    parts = [stats[side, :, i * T + blk * B : i * T + (blk + 1) * B] for i in range(3)]
    parts = jnp.concatenate(parts, axis=0)
    for h in range(2 * H):
        select = jnp.where(which == h, 1.0, 0.0).astype(BF)
        (lc, dc)[h // H][to, h % H * D : (h % H + 1) * D, :] = dot(parts, select, 0, 0)


def turn(rows, blk, qt, gt):
    for dst, first in ((qt, 0), (gt, B)):
        for h in range(H):
            cols = slice(h * D, (h + 1) * D)
            dst[blk, :, cols] = rows[blk, first : first + B, cols].T


def gather_kernel(
    k_ref, v_ref, q_ref, g_ref, o_ref, lse_ref, ka, va, rows, tail, stats, qt, gt, lc, dc, dk, dv,
    outs, lses, own_sem, s1, r1, s2, r2, s3, r3, ps, pr,
):
    z, y, x = coords()
    here = z * RING + x
    pair = ident(z, 1 - y, x)
    greet_signal(z, y, x)
    copies = []

    def keep(src, dst):
        copy = pltpu.make_async_copy(src, dst, own_sem.at[len(copies)])
        copy.start()
        copies.append(copy)

    first_rows, last_rows = pl.ds(0, B), pl.ds(B, B)
    keep(g_ref.at[first_rows], rows.at[0, last_rows])
    keep(g_ref.at[last_rows], rows.at[1, last_rows])
    keep(o_ref, outs)
    keep(lse_ref, lses)
    keep(q_ref.at[first_rows], rows.at[0, first_rows])
    keep(q_ref.at[last_rows], rows.at[1, first_rows])
    keep(q_ref.at[last_rows], tail.at[first_rows])
    keep(g_ref.at[last_rows], tail.at[last_rows])
    keep(k_ref, ka.at[here])
    keep(v_ref, va.at[here])
    greet_wait()

    def send(src, dst, ssem, rsem, to):
        copy = pltpu.make_async_remote_copy(
            src_ref=src, dst_ref=dst, send_sem=ssem, recv_sem=rsem, device_id=to, device_id_type=MESH
        )
        copy.start()
        return copy

    srcs, alls = (k_ref, v_ref), (ka, va)

    def first_peer(a, d):
        return ident(z, y, step_of(x, d)) if a == 0 else ident(step_of(z, d), y, x)

    def second_peer(a, d):
        return first_peer(1 - a, d)

    def slot_from(a, s, t=0):
        if a == 0:
            return step_of(z, RING - t) * RING + step_of(x, RING - s)
        return step_of(z, RING - s) * RING + step_of(x, RING - t)

    first, second, third = {}, {}, {}

    def spread(a, s):
        src = srcs[a] if s == 0 else alls[a].at[slot_from(a, s)]
        dst = alls[a].at[here if s == 0 else slot_from(a, s)]
        for e in (1, 3, 2) if s == 2 else (1, 3):
            second[a, s, e] = send(src, dst, s2.at[a, s, e - 1], r2.at[a, s, e - 1], second_peer(a, e))

    for d in (1, 3, 2):
        for a in (0, 1):
            first[a, d] = send(srcs[a], alls[a].at[here], s1.at[a, d - 1], r1.at[a, d - 1], first_peer(a, d))
    for a in (0, 1):
        spread(a, 0)
    across = [
        send(q_ref.at[first_rows], rows.at[2, first_rows], ps.at[0], pr.at[0], pair),
        send(g_ref.at[first_rows], rows.at[2, last_rows], ps.at[1], pr.at[1], pair),
    ]

    for copy in copies[:4]:
        copy.wait()
    ones = jnp.ones((8, D), BF)
    deltas = []
    for h in range(H):
        cols = slice(h * D, (h + 1) * D)
        grad = jnp.concatenate([rows[0, B:, cols], rows[1, B:, cols]], axis=0)
        prod = grad.astype(F32) * outs[:, cols].astype(F32)
        hi = prod.astype(BF)
        lo = (prod - hi.astype(F32)).astype(BF)
        deltas.append((dot(ones, hi, 1, 1) + dot(ones, lo, 1, 1))[0:1, :])
    whole = jnp.concatenate([jnp.minimum(lses[...], 1e30) * jnp.float32(LOG2E)] + deltas, axis=0)
    for i, piece in enumerate(pieces(whole)):
        stats[0, :, i * T : (i + 1) * T] = piece
    stats[0, :, 3 * T :] = jnp.zeros((2 * H, T), BF)
    across.append(send(stats.at[0], stats.at[1], ps.at[2], pr.at[2], pair))

    for s in (1, 3, 2):
        for a in (0, 1):
            first[a, s].wait_recv()
            spread(a, s)

    def relay(s):
        for e, half in ((1, 0), (3, 1)):
            for a in (0, 1):
                second[a, s, e].wait_recv()
                part = alls[a].at[slot_from(a, s, e), pl.ds(half * B, B)]
                third[a, s, half] = send(part, part, s3.at[a, s, half], r3.at[a, s, half], second_peer(a, e))

    dk[...] = jnp.zeros_like(dk)
    dv[...] = jnp.zeros_like(dv)
    relay(0)
    for copy in copies[4:]:
        copy.wait()
    relay(1)
    for blk in (0, 1):
        widen(stats, 0, blk, lc, dc, blk)
    relay(3)
    for blk in (0, 1):
        turn(rows, blk, qt, gt)
    for copy in across:
        copy.wait_recv()
    turn(rows, 2, qt, gt)
    widen(stats, 1, 0, lc, dc, 2)
    for a in (0, 1):
        for e in (1, 3, 2):
            second[a, 2, e].wait_recv()
    for copy in third.values():
        copy.wait_recv()
    for copy in list(first.values()) + list(second.values()) + list(third.values()) + across:
        copy.wait_send()


def gather(*arrays):
    dma = pltpu.SemaphoreType.DMA
    terms = pltpu.VMEM((3, H * B, D), F32)
    turned = pltpu.VMEM((3, D, H * B), BF)
    sums = pltpu.VMEM((2 * PLANE, D, B), F32)
    outs = (
        pltpu.VMEM((PLANE, T, D), BF),
        pltpu.VMEM((PLANE, T, D), BF),
        pltpu.VMEM((3, T, H * D), BF),
        pltpu.VMEM((T, H * D), BF),
        pltpu.VMEM((2, 2 * H, H * D), BF),
        turned, turned, terms, terms, sums, sums,
    )
    return pl.pallas_call(
        gather_kernel,
        out_shape=outs,
        in_specs=[ANY] * len(arrays),
        out_specs=(VM,) * len(outs),
        scratch_shapes=[
            pltpu.VMEM((T, H * D), BF),
            pltpu.VMEM((H, T), F32),
            dma((10,)), dma((2, 3)), dma((2, 3)), dma((2, 4, 3)), dma((2, 4, 3)),
            dma((2, 4, 2)), dma((2, 4, 2)), dma((3,)), dma((3,)),
        ],
        compiler_params=pltpu.CompilerParams(
            collective_id=0, has_side_effects=True, vmem_limit_bytes=VMEM_LIMIT
        ),
        name="gather_rows",
    )(*[stay(t) for t in arrays])


KEYS = 36
NEVER = 1 << 20


def attend_kernel(count, order, lens, *refs):
    early = count == 3
    if early:
        k_ref, v_ref, rows, qt, gt, lc, dc, _, _, dk, dv, dqa, dq_out = refs[:13]
        slots, places, qfrom, qbase, pbuf, dbuf = refs[13:]
    else:
        k_ref, v_ref, rows, stats, _, _, dk, dv, dq_out = refs[:9]
        slots, places, qfrom, qbase, pbuf, dbuf, qt, gt, lc, dc, dqa = refs[9:]
    me = lax.axis_index("ctx")
    plane = (me // 4) % 2
    mate = me + 4 - 8 * plane
    blocks = range(count)

    ats = [order[i] for i in ((me * 2, me * 2 + 1, mate * 2) if early else (mate * 2 + 1,))]
    row = lax.broadcasted_iota(I32, (B, D), 0)
    lows = [jnp.int32(0) for _ in blocks]
    begins = [jnp.zeros_like(row) for _ in blocks]
    end = jnp.int32(0)
    for d in range(lens.shape[0]):
        end = end + lens[d]
        for blk in blocks:
            lows[blk] = jnp.where(end <= ats[blk] * B, end, lows[blk])
            begins[blk] = jnp.where(end <= ats[blk] * B + row, end, begins[blk])
    lows = [low // B for low in lows]
    for blk in blocks:
        qfrom[blk] = begins[blk]
        qbase[blk] = ats[blk] * B

    def list_keys(i, counts):
        counts = list(counts)
        for j in range(8):
            slot = i * 8 + j
            p = order[i * 16 + plane * 8 + j]
            for blk in blocks:
                slots[blk * KEYS + counts[blk]] = slot
                places[blk * KEYS + counts[blk]] = p * B
                needed = (p >= lows[blk]) & (p <= ats[blk])
                counts[blk] = counts[blk] + needed.astype(I32)
        return tuple(counts)

    counts = lax.fori_loop(0, 4, list_keys, tuple(jnp.int32(0) for _ in blocks))
    for blk in blocks:
        slots[blk * KEYS + counts[blk]] = 0
        places[blk * KEYS + counts[blk]] = NEVER
    items = [(n + 1) // 2 for n in counts]
    total = sum(items[1:], items[0])

    dqa[...] = jnp.zeros_like(dqa)
    if not early:
        widen(stats, 1, 1, lc, dc, 0)
        turn(rows, 0, qt, gt)
    scale = jnp.float32(D**-0.5 * LOG2E)
    across = lax.broadcasted_iota(I32, (1, B), 1)

    def load(n):
        at, which, past = 2 * n, jnp.int32(0), jnp.int32(0)
        for blk in blocks[:-1]:
            past = past + items[blk]
            later = n >= past
            which = which + later.astype(I32)
            at = at + jnp.where(later, KEYS - 2 * items[blk], 0)
        a, b = slots[at], slots[at + 1]
        kk = jnp.concatenate([k_ref[a], k_ref[b]], axis=0)
        vv = jnp.concatenate([v_ref[a], v_ref[b]], axis=0)
        return which, a, b, kk, vv, places[at], places[at + 1]

    def scores(item, par):
        blk, _, _, kk, vv, place_a, place_b = item
        key_pos = jnp.concatenate([place_a + across, place_b + across], axis=1)
        here = qbase[blk] + row
        here = jnp.concatenate([here, here], axis=1)
        begin = qfrom[blk]
        begin = jnp.concatenate([begin, begin], axis=1)
        allowed = (key_pos <= here) & (key_pos >= begin)
        allowed = jnp.concatenate([allowed, allowed], axis=0)
        for two in range(4):
            cols = slice(two * 256, (two + 1) * 256)
            heads = [slice((2 * two + i) * D, (2 * two + i + 1) * D) for i in (0, 1)]
            score = dot(jnp.concatenate([rows[blk, :B, c] for c in heads], axis=0), kk, 1, 1)
            dprob = dot(jnp.concatenate([rows[blk, B:, c] for c in heads], axis=0), vv, 1, 1)
            less = lc[blk, cols, :]
            delta = dc[blk, cols, :]
            prob = jnp.where(allowed, jnp.exp2(score * scale - jnp.concatenate([less, less], axis=1)), 0.0)
            pbuf[par, cols, :] = prob.astype(BF)
            dbuf[par, cols, :] = (prob * (dprob - jnp.concatenate([delta, delta], axis=1))).astype(BF)

    def grads(item, par):
        blk, a, b, kk = item[:4]
        dqa[blk] += jnp.dot(dbuf[par], kk, preferred_element_type=F32)
        dv_term = jnp.dot(gt[blk], pbuf[par], preferred_element_type=F32)
        dk_term = jnp.dot(qt[blk], dbuf[par], preferred_element_type=F32)
        dk[a] += dk_term[:, :B]
        dk[b] += dk_term[:, B:]
        dv[a] += dv_term[:, :B]
        dv[b] += dv_term[:, B:]

    def two(i, c):
        now = [load(2 * i), load(2 * i + 1)]
        for par in (0, 1):
            scores(now[par], par)
        for par in (0, 1):
            grads(now[par], par)
        return c

    lax.fori_loop(0, total // 2, two, 0)

    @pl.when(total % 2 == 1)
    def _():
        last = load(total - 1)
        scores(last, 0)
        grads(last, 0)

    dq_out[...] = dqa[count - 1].astype(BF)


def attend(count, order, lens, *arrays):
    sums = pltpu.VMEM((2 * PLANE, D, B), F32)
    terms = pltpu.VMEM((count, H * B, D), F32)
    turned = pltpu.VMEM((count, D, H * B), BF)
    part = pltpu.VMEM((H * B, D), BF)
    scratch = [
        pltpu.SMEM((count * KEYS,), I32),
        pltpu.SMEM((count * KEYS,), I32),
        pltpu.VMEM((count, B, D), I32),
        pltpu.SMEM((count,), I32),
        pltpu.VMEM((2, H * B, 2 * B), BF),
        pltpu.VMEM((2, H * B, 2 * B), BF),
    ]
    if count == 3:
        outs = (sums, sums, terms, part)
    else:
        scratch += [turned, turned, terms, terms, terms]
        outs = (sums, sums, part)
    return pl.pallas_call(
        functools.partial(attend_kernel, count),
        out_shape=outs,
        in_specs=[SM] * 2 + [VM] * len(arrays),
        out_specs=(VM,) * len(outs),
        scratch_shapes=scratch,
        input_output_aliases={len(arrays): 0, len(arrays) + 1: 1},
        compiler_params=pltpu.CompilerParams(vmem_limit_bytes=VMEM_LIMIT),
        name="attend_early" if count == 3 else "attend_late",
    )(stay(order), stay(lens), *arrays)


def reduce_kernel(dq_early, dq_late, dk_ref, dv_ref, back, k_sum, v_sum, out1, in1, out_joint, in_side, out2, in2, s1, r1, s2, r2, ps, pr):
    z, y, x = coords()
    greet_signal(z, y, x)
    srcs = (dk_ref, dv_ref)
    for a in (0, 1):
        out1[a] = srcs[a][...].astype(BF)
    greet_wait()

    def send(src, dst, ssem, rsem, to):
        copy = pltpu.make_async_remote_copy(
            src_ref=src, dst_ref=dst, send_sem=ssem, recv_sem=rsem, device_id=to, device_id_type=MESH
        )
        copy.start()
        return copy

    def first_peer(a, d):
        return ident(step_of(z, d), y, x) if a == 0 else ident(z, y, step_of(x, d))

    def second_peer(a, e):
        return first_peer(1 - a, e)

    def slot(a, d, e):
        if a == 0:
            return step_of(z, d) * RING + step_of(x, e)
        return step_of(z, e) * RING + step_of(x, d)

    order, sides = (2, 1, 3, 0), ((1, 0), (3, 1))
    far, plain, joint, second = {}, {}, {}, {}
    for e in order:
        for a in (0, 1):
            for d, half in sides:
                far[a, e, half] = send(
                    out1.at[a, slot(a, 2, e), half], in1.at[a, e, half], s1.at[a, e, half], r1.at[a, e, half],
                    first_peer(a, d),
                )
    across = [
        send(src, back.at[blk], ps.at[blk], pr.at[blk], ident(z, 1 - y, x))
        for blk, src in enumerate((dq_early, dq_late))
    ]
    for e in order:
        for a in (0, 1):
            for d, half in sides:
                plain[a, e, half] = send(
                    out1.at[a, slot(a, d, e), 1 - half], in_side.at[a, e, half, 1 - half],
                    s1.at[a, e, 2 + half], r1.at[a, e, 2 + half], first_peer(a, d),
                )
        for a in (0, 1):
            for d, half in sides:
                far[a, e, half].wait_recv()
                both = srcs[a][slot(a, d, e), half] + in1[a, e, half].astype(F32)
                out_joint[a, e, half] = both.astype(BF)
                joint[a, e, half] = send(
                    out_joint.at[a, e, half], in_side.at[a, e, half, half],
                    s1.at[a, e, 4 + half], r1.at[a, e, 4 + half], first_peer(a, d),
                )
    sums = []
    for e in order:
        for a in (0, 1):
            for half in (0, 1):
                plain[a, e, half].wait_recv()
                joint[a, e, half].wait_recv()
            total = srcs[a][slot(a, 0, e)] + in_side[a, e, 0].astype(F32) + in_side[a, e, 1].astype(F32)
            if e:
                out2[a, e - 1] = total.astype(BF)
                second[a, e] = send(out2.at[a, e - 1], in2.at[a, e - 1], s2.at[a, e - 1], r2.at[a, e - 1], second_peer(a, e))
            else:
                sums.append(total)
    for a, dst in ((0, k_sum), (1, v_sum)):
        total = sums[a]
        for e in (1, 2, 3):
            second[a, e].wait_recv()
            total = total + in2[a, e - 1].astype(F32)
        dst[...] = total
    for copy in across:
        copy.wait()
    for copy in [*far.values(), *plain.values(), *joint.values(), *second.values()]:
        copy.wait_send()


def reduce(dq_early, dq_late, dk, dv):
    dma = pltpu.SemaphoreType.DMA
    return pl.pallas_call(
        reduce_kernel,
        out_shape=(
            pltpu.VMEM((2, H * B, D), BF),
            pltpu.VMEM((2, D, B), F32),
            pltpu.VMEM((2, D, B), F32),
        ),
        in_specs=[VM] * 4,
        out_specs=(VM,) * 3,
        scratch_shapes=[
            pltpu.VMEM((2, PLANE, 2, D, B), BF),
            pltpu.VMEM((2, 4, 2, D, B), BF),
            pltpu.VMEM((2, 4, 2, D, B), BF),
            pltpu.VMEM((2, 4, 2, 2, D, B), BF),
            pltpu.VMEM((2, 3, 2, D, B), BF),
            pltpu.VMEM((2, 3, 2, D, B), BF),
            dma((2, 4, 6)), dma((2, 4, 6)), dma((2, 3)), dma((2, 3)), dma((2,)), dma((2,)),
        ],
        compiler_params=pltpu.CompilerParams(
            collective_id=1, has_side_effects=True, vmem_limit_bytes=VMEM_LIMIT
        ),
        name="reduce_rows",
    )(dq_early, dq_late, dk.reshape(PLANE, 2, D, B), dv.reshape(PLANE, 2, D, B))


def finish_kernel(dq_own, back, k_sum, v_sum, query_ref, key_ref, value_ref):
    scale = jnp.float32(D**-0.5)
    for blk in (0, 1):
        rows = slice(blk * B, (blk + 1) * B)
        for h in range(H):
            cols = slice(h * D, (h + 1) * D)
            query_ref[rows, cols] = (scale * (dq_own[blk, cols, :] + back[blk, cols, :].astype(F32))).astype(BF)
        key_ref[rows, :] = (scale * k_sum[blk]).T.astype(BF)
        value_ref[rows, :] = v_sum[blk].T.astype(BF)


def finish(*arrays):
    grad = jax.ShapeDtypeStruct((T, D), BF)
    return pl.pallas_call(
        finish_kernel,
        out_shape=(jax.ShapeDtypeStruct((T, H * D), BF), grad, grad),
        in_specs=[VM] * 4,
        out_specs=(VM,) * 3,
        compiler_params=pltpu.CompilerParams(vmem_limit_bytes=VMEM_LIMIT),
        name="finish",
    )(*arrays)


def local(queries, keys, values, outputs, out_grad, lse, block_order, doc_lengths):
    swap = [(i, i ^ 4) for i in range(2 * PLANE)]
    ka, va, rows, tail, stats, qt, gt, lc, dc, dk, dv = gather(keys, values, queries, out_grad, outputs, lse)
    pair_tail = lax.ppermute(tail, "ctx", swap)
    k = ka.reshape(2 * PLANE, B, D)
    v = va.reshape(2 * PLANE, B, D)
    dk, dv, dq_own, dq_early = attend(3, block_order, doc_lengths, k, v, rows, qt, gt, lc, dc, dk, dv)
    pair_rows = pair_tail.reshape(1, T, H * D)
    dk, dv, dq_late = attend(1, block_order, doc_lengths, k, v, pair_rows, stats, dk, dv)
    back, k_sum, v_sum = reduce(dq_early, dq_late, dk, dv)
    return finish(dq_own, back, k_sum, v_sum)


def solution(mesh):
    rows = P(("dp", "ctx"), None)
    return jax.shard_map(
        local,
        mesh=mesh,
        in_specs=(rows, rows, rows, rows, rows, P(None, ("dp", "ctx")), P("dp"), P("dp")),
        out_specs=(rows, rows, rows),
        check_vma=False,
    )
```

time: 66.3 us -> 62.6 us (0.944)
  Pallas kernels: 61.4 us -> 58.6 us
  starting transfers between devices: 3.36 us -> 2.2 us
    pallas_call x4 -> x3, Pallas kernels: 38.3 us -> 35.4 us  [the longest x1 22.2 us: gather(): pl.pallas_call(gather_kernel, out_shape=outs, in_specs=[ANY] * len(arrays...]
    ppermute x1, starting transfers between devices: 3.36 us -> 2.2 us  [local(): pair_tail = lax.ppermute(tail, 'ctx', swap)]
  transfers between devices with their start and end apart: 1 -> 1, of which waited for: 0 -> 0; matrix products, arithmetic and copies ran while one was open for 0% -> 0% of each run, Pallas kernels for 43% -> 19%
where the time goes in v5:
time: 62.6 us; the launch traced here: 61.4 us
  Pallas kernels  58.6 us (94%)
  starting transfers between devices  2.2 us (4%)
  between operations  0.67 us (1%)
    pallas_call x1, Pallas kernels, gather(): pl.pallas_call(gather_kernel, out_shape=outs, in_specs=[ANY] * len(arrays...  22.2 us
    pallas_call x1, Pallas kernels, reduce(): pl.pallas_call(reduce_kernel, out_shape=(pltpu.VMEM((2, H * B, D), BF), p...  22.1 us
    pallas_call x2, Pallas kernels, attend(): pl.pallas_call(functools.partial(attend_kernel, count), out_shape=outs, i...  13.2 us
    ppermute x1, starting transfers between devices, local(): pair_tail = lax.ppermute(tail, 'ctx', swap)  2.2 us
  transfers between devices with their start and end apart: 1, of which 0 were waited for; matrix products, arithmetic and copies ran while one was open for 0% of the time, Pallas kernels for 19%

profile of v5, /device:TPU:0, one launch (start us, length us, event | category | flops | bytes accessed | tf_op | source)
XLA Modules:
  0.0 61.4 jit_solution(430194579933168358)
XLA Ops:
  0.6 22.2 %gather_rows.1 = (bf16[16,256,128]{2,1,0:T(8,128)(2,1)S(1)}, bf16[16,256,128]{2,1,0:T(8,128)(2,1)S(1)}, bf16[3,256,1024]{2,1,0:T(8,128)(2,1)S(1)}, bf16[256,1024...) custom-call(bf16[256,128]{1,0:T(8,128)(2,1)} %k_ref.1, ...), custom_call_target="tpu_custom_call" | custom-call | tf_op jit(solution)/shard_map/gather_rows/pallas_call | solution.py:218
  22.9 2.2 %collective-permute-start = (bf16[256,1024]{1,0:T(8,128)(2,1)S(1)}, bf16[256,1024]{1,0:T(8,128)(2,1)S(1)}, u32[]{:S(2)}, u32[]{:S(2)}) collective-permute-start(bf16[256,1024]{1,0:T(8,128)(2,1)S(1)} %get-tuple-element.35), channel_id=1, source_target_pairs={{0,16},{4,20},{8,24},{12,28},{16,0},{20,4},{24,8},{28,12},{32,48},... | collective-permute-start | bytes 1572872 | tf_op jit(solution)/shard_map/ppermute | solution.py:517
  25.1 11.9 %attend_early.1 = (f32[32,128,128]{2,1,0:T(8,128)S(1)}, f32[32,128,128]{2,1,0:T(8,128)S(1)}, f32[3,1024,128]{2,1,0:T(8,128)S(1)}, bf16[1024,128]{1,0:T(8,128)(2,1)S(1)}) custom-call(s32[64]{0:T(128)} %order.3, s32[16]{0:T(128)} %lens.3, bf16[32,128,128]{2,1,0:T(8,128)(2,1)S(1)} %bitcast.7, ...), custom_call_target="tpu_custom_call", output_to_operand_aliasing={{0}: (9, {}), {1}: (10, {})} | custom-call | tf_op jit(solution)/shard_map/attend_early/pallas_call | solution.py:373
  37.0 0.0 collective-permute-done
  37.0 1.3 %attend_late.1 = (f32[32,128,128]{2,1,0:T(8,128)S(1)}, f32[32,128,128]{2,1,0:T(8,128)S(1)}, bf16[1024,128]{1,0:T(8,128)(2,1)S(1)}) custom-call(s32[64]{0:T(128)} %order.3, s32[16]{0:T(128)} %lens.3, bf16[32,128,128]{2,1,0:T(8,128)(2,1)S(1)} %bitcast.8, bf16[32,128,128]{2,1,0:T(8,128)(2,1)S(1)} %bitcast.10, ...), custom_call_target="tpu_custom_call", output_to_operand_aliasing={{0}: (6, {}), {1}: (7, {})} | custom-call | tf_op jit(solution)/shard_map/attend_late/pallas_call | solution.py:373
  38.3 22.1 %reduce_rows.1 = (bf16[2,1024,128]{2,1,0:T(8,128)(2,1)S(1)}, f32[2,128,128]{2,1,0:T(8,128)S(1)}, f32[2,128,128]{2,1,0:T(8,128)S(1)}) custom-call(bf16[1024,128]{1,0:T(8,128)(2,1)S(1)} %get-tuple-element.34.dq_early, bf16[1024,128]{1,0:T(8,128)(2,1)S(1)} %get-tuple-element.39.dq_late, f32[16,2,128,128]{3,2,1,0:T(8,128)S(1)} %bitcast.5, ...), custom_call_target="tpu_custom_call" | custom-call | tf_op jit(solution)/shard_map/reduce_rows/pallas_call | solution.py:466
  60.4 1.0 %finish.1 = (bf16[256,1024]{1,0:T(8,128)(2,1)}, bf16[256,128]{1,0:T(8,128)(2,1)}, bf16[256,128]{1,0:T(8,128)(2,1)}) custom-call(f32[3,1024,128]{2,1,0:T(8,128)S(1)} %get-tuple-element.33.dq_own, bf16[2,1024,128]{2,1,0:T(8,128)(2,1)S(1)} %get-tuple-element.42.back, f32[2,128,128]{2,1,0:T(8,128)S(1)} %get-tuple-element.43.k_sum, ...), custom_call_target="tpu_custom_call" | custom-call | tf_op jit(solution)/shard_map/finish/pallas_call | solution.py:504
Async XLA Ops:
  22.9 14.2 %collective-permute-start = (bf16[256,1024]{1,0:T(8,128)(2,1)S(1)}, bf16[256,1024]{1,0:T(8,128)(2,1)S(1)}, u32[]{:S(2)}, u32[]{:S(2)}) collective-permute-start(bf16[256,1024]{1,0:T(8,128)(2,1)S(1)} %get-tuple-element.35), channel_id=1, source_target_pairs={{0,16},{4,20},{8,24},{12,28},{16,0},{20,4},{24,8},{28,12},{32,48},... | collective-permute-start | bytes 1572872 | tf_op jit(solution)/shard_map/ppermute | solution.py:517

commit v6 on v5

--- a/solution.py
+++ b/solution.py
@@ -166,10 +166,21 @@
     stats[0, :, 3 * T :] = jnp.zeros((2 * H, T), BF)
     across.append(send(stats.at[0], stats.at[1], ps.at[2], pr.at[2], pair))
 
-    for s in (1, 3, 2):
+    def forward(s):
         for a in (0, 1):
             first[a, s].wait_recv()
             spread(a, s)
+
+    forward(1)
+    forward(3)
+    forward(2)
+    dk[...] = jnp.zeros_like(dk)
+    dv[...] = jnp.zeros_like(dv)
+    for copy in copies[4:]:
+        copy.wait()
+    for blk in (0, 1):
+        widen(stats, 0, blk, lc, dc, blk)
+        turn(rows, blk, qt, gt)
 
     def relay(s):
         for e, half in ((1, 0), (3, 1)):
@@ -178,17 +189,9 @@
                 part = alls[a].at[slot_from(a, s, e), pl.ds(half * B, B)]
                 third[a, s, half] = send(part, part, s3.at[a, s, half], r3.at[a, s, half], second_peer(a, e))
 
-    dk[...] = jnp.zeros_like(dk)
-    dv[...] = jnp.zeros_like(dv)
     relay(0)
-    for copy in copies[4:]:
-        copy.wait()
     relay(1)
-    for blk in (0, 1):
-        widen(stats, 0, blk, lc, dc, blk)
     relay(3)
-    for blk in (0, 1):
-        turn(rows, blk, qt, gt)
     for copy in across:
         copy.wait_recv()
     turn(rows, 2, qt, gt)

time: 62.6 us -> 61.1 us (0.976); the launches traced: 61.4 us -> 60.6 us
  Pallas kernels: 58.6 us -> 51.1 us
  waiting for transfers between devices: 0.01 us -> 6.56 us
    pallas_call x2, Pallas kernels: 13.2 us -> 6.04 us  [attend(): pl.pallas_call(functools.partial(attend_kernel, count), out_shape=outs, i...]
    ppermute x1, waiting for transfers between devices: 0.01 us -> 6.56 us  [local(): pair_tail = lax.ppermute(tail, 'ctx', swap)]
  transfers between devices with their start and end apart: 1 -> 1, of which waited for: 0 -> 1; matrix products, arithmetic and copies ran while one was open for 0% -> 0% of each run, Pallas kernels for 19% -> 8%
where the time goes in v6:
time: 61.1 us; the launch traced here: 60.6 us
  Pallas kernels  51.1 us (84%)
  waiting for transfers between devices  6.56 us (11%)
  starting transfers between devices  2.2 us (4%)
  between operations  0.66 us (1%)
    pallas_call x1, Pallas kernels, gather(): pl.pallas_call(gather_kernel, out_shape=outs, in_specs=[ANY] * len(arrays...  22.2 us
    pallas_call x1, Pallas kernels, reduce(): pl.pallas_call(reduce_kernel, out_shape=(pltpu.VMEM((2, H * B, D), BF), p...  21.9 us
    ppermute x1, waiting for transfers between devices, local(): pair_tail = lax.ppermute(tail, 'ctx', swap)  6.56 us
    pallas_call x2, Pallas kernels, attend(): pl.pallas_call(functools.partial(attend_kernel, count), out_shape=outs, i...  6.04 us
    ppermute x1, starting transfers between devices, local(): pair_tail = lax.ppermute(tail, 'ctx', swap)  2.2 us
  transfers between devices with their start and end apart: 1, of which 1 were waited for; matrix products, arithmetic and copies ran while one was open for 0% of the time, Pallas kernels for 8%

profile of v6, /device:TPU:0, one launch (start us, length us, event | category | flops | bytes accessed | tf_op | source)
XLA Modules:
  0.0 60.6 jit_solution(1068067409025896820)
XLA Ops:
  0.6 22.2 %gather_rows.1 = (bf16[16,256,128]{2,1,0:T(8,128)(2,1)S(1)}, bf16[16,256,128]{2,1,0:T(8,128)(2,1)S(1)}, bf16[3,256,1024]{2,1,0:T(8,128)(2,1)S(1)}, bf16[256,1024...) custom-call(bf16[256,128]{1,0:T(8,128)(2,1)} %k_ref.1, ...), custom_call_target="tpu_custom_call" | custom-call | tf_op jit(solution)/shard_map/gather_rows/pallas_call | solution.py:221
  22.9 2.2 %collective-permute-start = (bf16[256,1024]{1,0:T(8,128)(2,1)S(1)}, bf16[256,1024]{1,0:T(8,128)(2,1)S(1)}, u32[]{:S(2)}, u32[]{:S(2)}) collective-permute-start(bf16[256,1024]{1,0:T(8,128)(2,1)S(1)} %get-tuple-element.35), channel_id=1, source_target_pairs={{0,16},{4,20},{8,24},{12,28},{16,0},{20,4},{24,8},{28,12},{32,48},... | collective-permute-start | bytes 1572872 | tf_op jit(solution)/shard_map/ppermute | solution.py:520
  25.1 4.8 %attend_early.1 = (f32[32,128,128]{2,1,0:T(8,128)S(1)}, f32[32,128,128]{2,1,0:T(8,128)S(1)}, f32[3,1024,128]{2,1,0:T(8,128)S(1)}, bf16[1024,128]{1,0:T(8,128)(2,1)S(1)}) custom-call(s32[64]{0:T(128)} %order.3, s32[16]{0:T(128)} %lens.3, bf16[32,128,128]{2,1,0:T(8,128)(2,1)S(1)} %bitcast.7, ...), custom_call_target="tpu_custom_call", output_to_operand_aliasing={{0}: (9, {}), {1}: (10, {})} | custom-call | tf_op jit(solution)/shard_map/attend_early/pallas_call | solution.py:376
  29.9 6.6 %collective-permute-done = bf16[256,1024]{1,0:T(8,128)(2,1)S(1)} collective-permute-done((bf16[256,1024]{1,0:T(8,128)(2,1)S(1)}, bf16[256,1024]{1,0:T(8,128)(2,1)S(1)}, u32[]{:S(2)}, u32[]{:S(2)}) %collective-permute-start) | collective-permute-done | bytes 524320 | tf_op jit(solution)/shard_map/ppermute | solution.py:520
  36.4 1.3 %attend_late.1 = (f32[32,128,128]{2,1,0:T(8,128)S(1)}, f32[32,128,128]{2,1,0:T(8,128)S(1)}, bf16[1024,128]{1,0:T(8,128)(2,1)S(1)}) custom-call(s32[64]{0:T(128)} %order.3, s32[16]{0:T(128)} %lens.3, bf16[32,128,128]{2,1,0:T(8,128)(2,1)S(1)} %bitcast.8, bf16[32,128,128]{2,1,0:T(8,128)(2,1)S(1)} %bitcast.10, ...), custom_call_target="tpu_custom_call", output_to_operand_aliasing={{0}: (6, {}), {1}: (7, {})} | custom-call | tf_op jit(solution)/shard_map/attend_late/pallas_call | solution.py:376
  37.7 21.9 %reduce_rows.1 = (bf16[2,1024,128]{2,1,0:T(8,128)(2,1)S(1)}, f32[2,128,128]{2,1,0:T(8,128)S(1)}, f32[2,128,128]{2,1,0:T(8,128)S(1)}) custom-call(bf16[1024,128]{1,0:T(8,128)(2,1)S(1)} %get-tuple-element.34.dq_early, bf16[1024,128]{1,0:T(8,128)(2,1)S(1)} %get-tuple-element.39.dq_late, f32[16,2,128,128]{3,2,1,0:T(8,128)S(1)} %bitcast.5, ...), custom_call_target="tpu_custom_call" | custom-call | tf_op jit(solution)/shard_map/reduce_rows/pallas_call | solution.py:469
  59.6 1.0 %finish.1 = (bf16[256,1024]{1,0:T(8,128)(2,1)}, bf16[256,128]{1,0:T(8,128)(2,1)}, bf16[256,128]{1,0:T(8,128)(2,1)}) custom-call(f32[3,1024,128]{2,1,0:T(8,128)S(1)} %get-tuple-element.33.dq_own, bf16[2,1024,128]{2,1,0:T(8,128)(2,1)S(1)} %get-tuple-element.42.back, f32[2,128,128]{2,1,0:T(8,128)S(1)} %get-tuple-element.43.k_sum, ...), custom_call_target="tpu_custom_call" | custom-call | tf_op jit(solution)/shard_map/finish/pallas_call | solution.py:507
Async XLA Ops:
  22.9 13.5 %collective-permute-start = (bf16[256,1024]{1,0:T(8,128)(2,1)S(1)}, bf16[256,1024]{1,0:T(8,128)(2,1)S(1)}, u32[]{:S(2)}, u32[]{:S(2)}) collective-permute-start(bf16[256,1024]{1,0:T(8,128)(2,1)S(1)} %get-tuple-element.35), channel_id=1, source_target_pairs={{0,16},{4,20},{8,24},{12,28},{16,0},{20,4},{24,8},{28,12},{32,48},... | collective-permute-start | bytes 1572872 | tf_op jit(solution)/shard_map/ppermute | solution.py:520

commit v7 on v6

--- a/solution.py
+++ b/solution.py
@@ -244,10 +244,10 @@
     early = count == 3
     if early:
         k_ref, v_ref, rows, qt, gt, lc, dc, _, _, dk, dv, dqa, dq_out = refs[:13]
-        slots, places, qfrom, qbase, pbuf, dbuf = refs[13:]
+        slots, places, qfrom, qbase, qlast, pbuf, dbuf = refs[13:]
     else:
         k_ref, v_ref, rows, stats, _, _, dk, dv, dq_out = refs[:9]
-        slots, places, qfrom, qbase, pbuf, dbuf, qt, gt, lc, dc, dqa = refs[9:]
+        slots, places, qfrom, qbase, qlast, pbuf, dbuf, qt, gt, lc, dc, dqa = refs[9:]
     me = lax.axis_index("ctx")
     plane = (me // 4) % 2
     mate = me + 4 - 8 * plane
@@ -256,17 +256,20 @@
     ats = [order[i] for i in ((me * 2, me * 2 + 1, mate * 2) if early else (mate * 2 + 1,))]
     row = lax.broadcasted_iota(I32, (B, D), 0)
     lows = [jnp.int32(0) for _ in blocks]
+    lasts = [jnp.int32(0) for _ in blocks]
     begins = [jnp.zeros_like(row) for _ in blocks]
     end = jnp.int32(0)
     for d in range(lens.shape[0]):
         end = end + lens[d]
         for blk in blocks:
             lows[blk] = jnp.where(end <= ats[blk] * B, end, lows[blk])
+            lasts[blk] = jnp.where(end <= ats[blk] * B + B - 1, end, lasts[blk])
             begins[blk] = jnp.where(end <= ats[blk] * B + row, end, begins[blk])
     lows = [low // B for low in lows]
     for blk in blocks:
         qfrom[blk] = begins[blk]
         qbase[blk] = ats[blk] * B
+        qlast[blk] = lasts[blk]
 
     def list_keys(i, counts):
         counts = list(counts)
@@ -306,7 +309,7 @@
         vv = jnp.concatenate([v_ref[a], v_ref[b]], axis=0)
         return which, a, b, kk, vv, places[at], places[at + 1]
 
-    def scores(item, par):
+    def scores(item, par, masked=True):
         blk, _, _, kk, vv, place_a, place_b = item
         key_pos = jnp.concatenate([place_a + across, place_b + across], axis=1)
         here = qbase[blk] + row
@@ -322,7 +325,9 @@
             dprob = dot(jnp.concatenate([rows[blk, B:, c] for c in heads], axis=0), vv, 1, 1)
             less = lc[blk, cols, :]
             delta = dc[blk, cols, :]
-            prob = jnp.where(allowed, jnp.exp2(score * scale - jnp.concatenate([less, less], axis=1)), 0.0)
+            prob = jnp.exp2(score * scale - jnp.concatenate([less, less], axis=1))
+            if masked:
+                prob = jnp.where(allowed, prob, 0.0)
             pbuf[par, cols, :] = prob.astype(BF)
             dbuf[par, cols, :] = (prob * (dprob - jnp.concatenate([delta, delta], axis=1))).astype(BF)
 
@@ -338,10 +343,20 @@
 
     def two(i, c):
         now = [load(2 * i), load(2 * i + 1)]
-        for par in (0, 1):
-            scores(now[par], par)
-        for par in (0, 1):
-            grads(now[par], par)
+        open_ = None
+        for blk, _, _, _, _, place_a, place_b in now:
+            low = jnp.minimum(place_a, place_b) >= qlast[blk]
+            high = jnp.maximum(place_a, place_b) < qbase[blk]
+            open_ = low & high if open_ is None else open_ & low & high
+
+        def run(masked):
+            for par in (0, 1):
+                scores(now[par], par, masked)
+            for par in (0, 1):
+                grads(now[par], par)
+
+        pl.when(open_)(lambda: run(False))
+        pl.when(jnp.logical_not(open_))(lambda: run(True))
         return c
 
     lax.fori_loop(0, total // 2, two, 0)
@@ -364,6 +379,7 @@
         pltpu.SMEM((count * KEYS,), I32),
         pltpu.SMEM((count * KEYS,), I32),
         pltpu.VMEM((count, B, D), I32),
+        pltpu.SMEM((count,), I32),
         pltpu.SMEM((count,), I32),
         pltpu.VMEM((2, H * B, 2 * B), BF),
         pltpu.VMEM((2, H * B, 2 * B), BF),

time: 61.1 us -> 60.7 us (level)
  Pallas kernels: 51.1 us -> 53.1 us
  waiting for transfers between devices: 6.56 us -> 4.61 us
    pallas_call x2, Pallas kernels: 6.04 us -> 7.99 us  [attend(): pl.pallas_call(functools.partial(attend_kernel, count), out_shape=outs, i...]
    ppermute x1, waiting for transfers between devices: 6.56 us -> 4.61 us  [local(): pair_tail = lax.ppermute(tail, 'ctx', swap)]
  transfers between devices with their start and end apart: 1 -> 1, of which waited for: 1 -> 1; matrix products, arithmetic and copies ran while one was open for 0% -> 0% of each run, Pallas kernels for 8% -> 11%
where the time goes in v7:
time: 60.7 us; the launch traced here: 60.5 us
  Pallas kernels  53.1 us (87%)
  waiting for transfers between devices  4.61 us (8%)
  starting transfers between devices  2.2 us (4%)
  between operations  0.66 us (1%)
    pallas_call x1, Pallas kernels, gather(): pl.pallas_call(gather_kernel, out_shape=outs, in_specs=[ANY] * len(arrays...  22.2 us
    pallas_call x1, Pallas kernels, reduce(): pl.pallas_call(reduce_kernel, out_shape=(pltpu.VMEM((2, H * B, D), BF), p...  21.8 us
    pallas_call x2, Pallas kernels, attend(): pl.pallas_call(functools.partial(attend_kernel, count), out_shape=outs, i...  7.99 us
    ppermute x1, waiting for transfers between devices, local(): pair_tail = lax.ppermute(tail, 'ctx', swap)  4.61 us
    ppermute x1, starting transfers between devices, local(): pair_tail = lax.ppermute(tail, 'ctx', swap)  2.2 us
  transfers between devices with their start and end apart: 1, of which 1 were waited for; matrix products, arithmetic and copies ran while one was open for 0% of the time, Pallas kernels for 11%

profile of v7, /device:TPU:0, one launch (start us, length us, event | category | flops | bytes accessed | tf_op | source)
XLA Modules:
  0.0 60.5 jit_solution(3945331727443537425)
XLA Ops:
  0.6 22.2 %gather_rows.1 = (bf16[16,256,128]{2,1,0:T(8,128)(2,1)S(1)}, bf16[16,256,128]{2,1,0:T(8,128)(2,1)S(1)}, bf16[3,256,1024]{2,1,0:T(8,128)(2,1)S(1)}, bf16[256,1024...) custom-call(bf16[256,128]{1,0:T(8,128)(2,1)} %k_ref.1, ...), custom_call_target="tpu_custom_call" | custom-call | tf_op jit(solution)/shard_map/gather_rows/pallas_call | solution.py:221
  22.9 2.2 %collective-permute-start = (bf16[256,1024]{1,0:T(8,128)(2,1)S(1)}, bf16[256,1024]{1,0:T(8,128)(2,1)S(1)}, u32[]{:S(2)}, u32[]{:S(2)}) collective-permute-start(bf16[256,1024]{1,0:T(8,128)(2,1)S(1)} %get-tuple-element.35), channel_id=1, source_target_pairs={{0,16},{4,20},{8,24},{12,28},{16,0},{20,4},{24,8},{28,12},{32,48},... | collective-permute-start | bytes 1572872 | tf_op jit(solution)/shard_map/ppermute | solution.py:536
  25.1 6.7 %attend_early.1 = (f32[32,128,128]{2,1,0:T(8,128)S(1)}, f32[32,128,128]{2,1,0:T(8,128)S(1)}, f32[3,1024,128]{2,1,0:T(8,128)S(1)}, bf16[1024,128]{1,0:T(8,128)(2,1)S(1)}) custom-call(s32[64]{0:T(128)} %order.3, s32[16]{0:T(128)} %lens.3, bf16[32,128,128]{2,1,0:T(8,128)(2,1)S(1)} %bitcast.7, ...), custom_call_target="tpu_custom_call", output_to_operand_aliasing={{0}: (9, {}), {1}: (10, {})} | custom-call | tf_op jit(solution)/shard_map/attend_early/pallas_call | solution.py:392
  31.8 4.6 %collective-permute-done = bf16[256,1024]{1,0:T(8,128)(2,1)S(1)} collective-permute-done((bf16[256,1024]{1,0:T(8,128)(2,1)S(1)}, bf16[256,1024]{1,0:T(8,128)(2,1)S(1)}, u32[]{:S(2)}, u32[]{:S(2)}) %collective-permute-start) | collective-permute-done | bytes 524320 | tf_op jit(solution)/shard_map/ppermute | solution.py:536
  36.4 1.3 %attend_late.1 = (f32[32,128,128]{2,1,0:T(8,128)S(1)}, f32[32,128,128]{2,1,0:T(8,128)S(1)}, bf16[1024,128]{1,0:T(8,128)(2,1)S(1)}) custom-call(s32[64]{0:T(128)} %order.3, s32[16]{0:T(128)} %lens.3, bf16[32,128,128]{2,1,0:T(8,128)(2,1)S(1)} %bitcast.8, bf16[32,128,128]{2,1,0:T(8,128)(2,1)S(1)} %bitcast.10, ...), custom_call_target="tpu_custom_call", output_to_operand_aliasing={{0}: (6, {}), {1}: (7, {})} | custom-call | tf_op jit(solution)/shard_map/attend_late/pallas_call | solution.py:392
  37.7 21.8 %reduce_rows.1 = (bf16[2,1024,128]{2,1,0:T(8,128)(2,1)S(1)}, f32[2,128,128]{2,1,0:T(8,128)S(1)}, f32[2,128,128]{2,1,0:T(8,128)S(1)}) custom-call(bf16[1024,128]{1,0:T(8,128)(2,1)S(1)} %get-tuple-element.34.dq_early, bf16[1024,128]{1,0:T(8,128)(2,1)S(1)} %get-tuple-element.39.dq_late, f32[16,2,128,128]{3,2,1,0:T(8,128)S(1)} %bitcast.5, ...), custom_call_target="tpu_custom_call" | custom-call | tf_op jit(solution)/shard_map/reduce_rows/pallas_call | solution.py:485
  59.5 1.0 %finish.1 = (bf16[256,1024]{1,0:T(8,128)(2,1)}, bf16[256,128]{1,0:T(8,128)(2,1)}, bf16[256,128]{1,0:T(8,128)(2,1)}) custom-call(f32[3,1024,128]{2,1,0:T(8,128)S(1)} %get-tuple-element.33.dq_own, bf16[2,1024,128]{2,1,0:T(8,128)(2,1)S(1)} %get-tuple-element.42.back, f32[2,128,128]{2,1,0:T(8,128)S(1)} %get-tuple-element.43.k_sum, ...), custom_call_target="tpu_custom_call" | custom-call | tf_op jit(solution)/shard_map/finish/pallas_call | solution.py:523
Async XLA Ops:
  22.9 13.5 %collective-permute-start = (bf16[256,1024]{1,0:T(8,128)(2,1)S(1)}, bf16[256,1024]{1,0:T(8,128)(2,1)S(1)}, u32[]{:S(2)}, u32[]{:S(2)}) collective-permute-start(bf16[256,1024]{1,0:T(8,128)(2,1)S(1)} %get-tuple-element.35), channel_id=1, source_target_pairs={{0,16},{4,20},{8,24},{12,28},{16,0},{20,4},{24,8},{28,12},{32,48},... | collective-permute-start | bytes 1572872 | tf_op jit(solution)/shard_map/ppermute | solution.py:536

commit v8 on v6

--- a/solution.py
+++ b/solution.py
@@ -118,6 +118,11 @@
         copy.start()
         return copy
 
+    across = [
+        send(q_ref.at[first_rows], rows.at[2, first_rows], ps.at[0], pr.at[0], pair),
+        send(g_ref.at[first_rows], rows.at[2, last_rows], ps.at[1], pr.at[1], pair),
+    ]
+
     srcs, alls = (k_ref, v_ref), (ka, va)
 
     def first_peer(a, d):
@@ -144,10 +149,6 @@
             first[a, d] = send(srcs[a], alls[a].at[here], s1.at[a, d - 1], r1.at[a, d - 1], first_peer(a, d))
     for a in (0, 1):
         spread(a, 0)
-    across = [
-        send(q_ref.at[first_rows], rows.at[2, first_rows], ps.at[0], pr.at[0], pair),
-        send(g_ref.at[first_rows], rows.at[2, last_rows], ps.at[1], pr.at[1], pair),
-    ]
 
     for copy in copies[:4]:
         copy.wait()

time: 61.1 us -> 61.1 us (level)
  waiting for transfers between devices: 6.56 us -> 7.32 us
  Pallas kernels: 51.1 us -> 50.4 us
    pallas_call x1, Pallas kernels: 21.9 us -> 20.6 us  [reduce(): pl.pallas_call(reduce_kernel, out_shape=(pltpu.VMEM((2, H * B, D), BF), p...]
    ppermute x1, waiting for transfers between devices: 6.56 us -> 7.32 us  [local(): pair_tail = lax.ppermute(tail, 'ctx', swap)]
  transfers between devices with their start and end apart: 1 -> 1, of which waited for: 1 -> 1; matrix products, arithmetic and copies ran while one was open for 0% -> 0% of each run, Pallas kernels for 8% -> 7%
where the time goes in v8:
time: 61.1 us; the launch traced here: 60.6 us
  Pallas kernels  50.4 us (82%)
  waiting for transfers between devices  7.32 us (12%)
  starting transfers between devices  2.2 us (4%)
  between operations  0.66 us (1%)
    pallas_call x1, Pallas kernels, gather(): pl.pallas_call(gather_kernel, out_shape=outs, in_specs=[ANY] * len(arrays...  22.2 us
    pallas_call x1, Pallas kernels, reduce(): pl.pallas_call(reduce_kernel, out_shape=(pltpu.VMEM((2, H * B, D), BF), p...  20.6 us
    ppermute x1, waiting for transfers between devices, local(): pair_tail = lax.ppermute(tail, 'ctx', swap)  7.32 us
    pallas_call x2, Pallas kernels, attend(): pl.pallas_call(functools.partial(attend_kernel, count), out_shape=outs, i...  6.59 us
    ppermute x1, starting transfers between devices, local(): pair_tail = lax.ppermute(tail, 'ctx', swap)  2.2 us
  transfers between devices with their start and end apart: 1, of which 1 were waited for; matrix products, arithmetic and copies ran while one was open for 0% of the time, Pallas kernels for 7%

profile of v8, /device:TPU:0, one launch (start us, length us, event | category | flops | bytes accessed | tf_op | source)
XLA Modules:
  0.0 60.6 jit_solution(166376953785982233)
XLA Ops:
  0.6 22.2 %gather_rows.1 = (bf16[16,256,128]{2,1,0:T(8,128)(2,1)S(1)}, bf16[16,256,128]{2,1,0:T(8,128)(2,1)S(1)}, bf16[3,256,1024]{2,1,0:T(8,128)(2,1)S(1)}, bf16[256,1024...) custom-call(bf16[256,128]{1,0:T(8,128)(2,1)} %k_ref.1, ...), custom_call_target="tpu_custom_call" | custom-call | tf_op jit(solution)/shard_map/gather_rows/pallas_call | solution.py:222
  22.9 2.2 %collective-permute-start = (bf16[256,1024]{1,0:T(8,128)(2,1)S(1)}, bf16[256,1024]{1,0:T(8,128)(2,1)S(1)}, u32[]{:S(2)}, u32[]{:S(2)}) collective-permute-start(bf16[256,1024]{1,0:T(8,128)(2,1)S(1)} %get-tuple-element.35), channel_id=1, source_target_pairs={{0,16},{4,20},{8,24},{12,28},{16,0},{20,4},{24,8},{28,12},{32,48},... | collective-permute-start | bytes 1572872 | tf_op jit(solution)/shard_map/ppermute | solution.py:521
  25.1 4.0 %attend_early.1 = (f32[32,128,128]{2,1,0:T(8,128)S(1)}, f32[32,128,128]{2,1,0:T(8,128)S(1)}, f32[3,1024,128]{2,1,0:T(8,128)S(1)}, bf16[1024,128]{1,0:T(8,128)(2,1)S(1)}) custom-call(s32[64]{0:T(128)} %order.3, s32[16]{0:T(128)} %lens.3, bf16[32,128,128]{2,1,0:T(8,128)(2,1)S(1)} %bitcast.7, ...), custom_call_target="tpu_custom_call", output_to_operand_aliasing={{0}: (9, {}), {1}: (10, {})} | custom-call | tf_op jit(solution)/shard_map/attend_early/pallas_call | solution.py:377
  29.1 7.3 %collective-permute-done = bf16[256,1024]{1,0:T(8,128)(2,1)S(1)} collective-permute-done((bf16[256,1024]{1,0:T(8,128)(2,1)S(1)}, bf16[256,1024]{1,0:T(8,128)(2,1)S(1)}, u32[]{:S(2)}, u32[]{:S(2)}) %collective-permute-start) | collective-permute-done | bytes 524320 | tf_op jit(solution)/shard_map/ppermute | solution.py:521
  36.4 2.6 %attend_late.1 = (f32[32,128,128]{2,1,0:T(8,128)S(1)}, f32[32,128,128]{2,1,0:T(8,128)S(1)}, bf16[1024,128]{1,0:T(8,128)(2,1)S(1)}) custom-call(s32[64]{0:T(128)} %order.3, s32[16]{0:T(128)} %lens.3, bf16[32,128,128]{2,1,0:T(8,128)(2,1)S(1)} %bitcast.8, bf16[32,128,128]{2,1,0:T(8,128)(2,1)S(1)} %bitcast.10, ...), custom_call_target="tpu_custom_call", output_to_operand_aliasing={{0}: (6, {}), {1}: (7, {})} | custom-call | tf_op jit(solution)/shard_map/attend_late/pallas_call | solution.py:377
  39.0 20.6 %reduce_rows.1 = (bf16[2,1024,128]{2,1,0:T(8,128)(2,1)S(1)}, f32[2,128,128]{2,1,0:T(8,128)S(1)}, f32[2,128,128]{2,1,0:T(8,128)S(1)}) custom-call(bf16[1024,128]{1,0:T(8,128)(2,1)S(1)} %get-tuple-element.34.dq_early, bf16[1024,128]{1,0:T(8,128)(2,1)S(1)} %get-tuple-element.39.dq_late, f32[16,2,128,128]{3,2,1,0:T(8,128)S(1)} %bitcast.5, ...), custom_call_target="tpu_custom_call" | custom-call | tf_op jit(solution)/shard_map/reduce_rows/pallas_call | solution.py:470
  59.6 1.0 %finish.1 = (bf16[256,1024]{1,0:T(8,128)(2,1)}, bf16[256,128]{1,0:T(8,128)(2,1)}, bf16[256,128]{1,0:T(8,128)(2,1)}) custom-call(f32[3,1024,128]{2,1,0:T(8,128)S(1)} %get-tuple-element.33.dq_own, bf16[2,1024,128]{2,1,0:T(8,128)(2,1)S(1)} %get-tuple-element.42.back, f32[2,128,128]{2,1,0:T(8,128)S(1)} %get-tuple-element.43.k_sum, ...), custom_call_target="tpu_custom_call" | custom-call | tf_op jit(solution)/shard_map/finish/pallas_call | solution.py:508
Async XLA Ops:
  22.9 13.5 %collective-permute-start = (bf16[256,1024]{1,0:T(8,128)(2,1)S(1)}, bf16[256,1024]{1,0:T(8,128)(2,1)S(1)}, u32[]{:S(2)}, u32[]{:S(2)}) collective-permute-start(bf16[256,1024]{1,0:T(8,128)(2,1)S(1)} %get-tuple-element.35), channel_id=1, source_target_pairs={{0,16},{4,20},{8,24},{12,28},{16,0},{20,4},{24,8},{28,12},{32,48},... | collective-permute-start | bytes 1572872 | tf_op jit(solution)/shard_map/ppermute | solution.py:521
